TPU v7x, 256 devices: a whole 4x4x8 slice. The times are simulated.
256 devices in a mesh: psg: 32 (over z, y), pb: 8 (over x, core).
Axes of the slice: x: 4, y: 4, z: 8, core: 2. Of those that a mesh axis runs over, the one named last changes fastest.
Arguments:
- dec_hidden: bfloat16 [8, 32, 4096], P('pb', None, 'psg'), may hold values from -6 to 6
- out_grad: bfloat16 [8, 32, 4096], P('pb', None, 'psg'), may hold values from -6 to 6
- query_weight: bfloat16 [4096, 2048], P('psg'), may hold values from -0.09375 to 0.09375
- output_weight: bfloat16 [2048, 4096], P(None, 'psg'), may hold values from -0.125 to 0.125
- queries: bfloat16 [8, 32, 2048], P('pb', 'psg'), may hold values from -3 to 3
- attn_out: bfloat16 [8, 32, 2048], P('pb', 'psg'), may hold values from -3 to 3
- row_max: float32 [8, 32, 32], P('pb', 'psg'), as said below
- row_sum: float32 [8, 32, 32], P('pb', 'psg'), as said below
- keys: bfloat16 [8, 64, 256, 2048], P('pb', 'psg'), may hold values from -2 to 2
- values: bfloat16 [8, 64, 256, 2048], P('pb', 'psg'), may hold values from -6 to 6
- lengths: int32 [8, 64], P('pb', 'psg'), may hold values from 1 to 256, as said below
Outputs:
- hidden_grad: bfloat16 [8, 32, 4096], P('pb', None, 'psg')
- key_grad: bfloat16 [8, 64, 256, 2048], P('pb', 'psg')
- value_grad: bfloat16 [8, 64, 256, 2048], P('pb', 'psg')
- query_weight_grad: float32 [4096, 2048], P('psg')
- output_weight_grad: float32 [2048, 4096], P(None, 'psg')
Inputs may be any that keep to these rules, and one draw needn't show every extreme that they name: row_max and row_sum are the maximum of scores over the valid slots of all the question's passages and the sum of exp(scores - row_max) over them, for each token and head. `row_max`: see row_sum. `lengths`: 256 is reached in every question.
All inputs are finite; a program needn't handle non-finite values.
Results may differ from a plain program's by a relative error of at most 0.0065.
Values may be sent and summed in bfloat16 or wider, within the bound.
A program may use at most 64 MiB of HBM per device.

v0:
```python
import jax
import jax.numpy as jnp
from jax import lax
from jax.sharding import PartitionSpec as P


def head_delta(grad_rows, out_rows, heads):
    product = grad_rows.astype(jnp.float32) * out_rows.astype(jnp.float32)
    shape = product.shape
    return jnp.sum(product.reshape(shape[0], shape[1], heads, shape[2] // heads), axis=3)


def local(
    dec_hidden,
    out_grad,
    query_weight,
    output_weight,
    queries,
    attn_out,
    row_max,
    row_sum,
    keys,
    values,
    lengths,
):
    heads = row_max.shape[2]
    width = queries.shape[2]
    head_dim = width // heads
    partial_value = jnp.einsum(
        "btc,ec->bte", out_grad, output_weight, preferred_element_type=jnp.float32
    )
    grad_rows = lax.psum_scatter(partial_value, "psg", scatter_dimension=1, tiled=True).astype(
        jnp.bfloat16
    )
    delta_rows = head_delta(grad_rows, attn_out, heads)
    query_all, out_all, grad_all, delta_all, max_all, sum_all = (
        lax.all_gather(queries.astype(jnp.float32), "psg", axis=1, tiled=True),
        lax.all_gather(attn_out.astype(jnp.float32), "psg", axis=1, tiled=True),
        lax.all_gather(grad_rows.astype(jnp.float32), "psg", axis=1, tiled=True),
        lax.all_gather(delta_rows, "psg", axis=1, tiled=True),
        lax.all_gather(row_max, "psg", axis=1, tiled=True),
        lax.all_gather(row_sum, "psg", axis=1, tiled=True),
    )
    grad_all = grad_all.astype(jnp.bfloat16)
    query_all = query_all.astype(jnp.bfloat16)
    out_all = out_all.astype(jnp.bfloat16)
    batch, dec = (query_all.shape[0], query_all.shape[1])
    local_psg, plen = (keys.shape[1], keys.shape[2])
    slots = local_psg * plen
    query_heads = query_all.reshape(batch, dec, heads, head_dim)
    grad_heads = grad_all.reshape(batch, dec, heads, head_dim)
    key_heads = keys.reshape(batch, slots, heads, head_dim)
    value_heads = values.reshape(batch, slots, heads, head_dim)
    scores = jnp.einsum(
        "bthd,bshd->bhts", query_heads, key_heads, preferred_element_type=jnp.float32
    )
    position = lax.broadcasted_iota(jnp.int32, (local_psg, plen), 1)
    valid_mask = (position[None] < lengths[:, :, None]).reshape(batch, 1, 1, slots)
    stat_max = jnp.transpose(max_all, (0, 2, 1))[..., None]
    stat_sum = jnp.transpose(sum_all, (0, 2, 1))[..., None]
    stat_delta = jnp.transpose(delta_all, (0, 2, 1))[..., None]
    attn_probs = jnp.where(valid_mask, jnp.exp(scores - stat_max), 0.0) / stat_sum
    probs_low = attn_probs.astype(jnp.bfloat16)
    value_grad = jnp.einsum(
        "bhts,bthd->bshd", probs_low, grad_heads, preferred_element_type=jnp.float32
    )
    value_grad = value_grad.astype(jnp.bfloat16).reshape(batch, local_psg, plen, width)
    prob_grad = jnp.einsum(
        "bthd,bshd->bhts", grad_heads, value_heads, preferred_element_type=jnp.float32
    )
    score_grad = (attn_probs * (prob_grad - stat_delta)).astype(jnp.bfloat16)
    key_grad = jnp.einsum(
        "bhts,bthd->bshd", score_grad, query_heads, preferred_element_type=jnp.float32
    )
    key_grad = key_grad.astype(jnp.bfloat16).reshape(batch, local_psg, plen, width)
    query_part = jnp.einsum(
        "bhts,bshd->bthd", score_grad, key_heads, preferred_element_type=jnp.float32
    )
    query_part = query_part.reshape(batch, dec, width)
    query_rows = lax.psum_scatter(query_part, "psg", scatter_dimension=1, tiled=True).astype(
        jnp.bfloat16
    )
    query_grad = lax.all_gather(query_rows, "psg", axis=1, tiled=True)
    hidden_grad = jnp.einsum(
        "bte,ce->btc", query_grad, query_weight, preferred_element_type=jnp.float32
    ).astype(jnp.bfloat16)
    local_query = jnp.einsum(
        "btc,bte->ce", dec_hidden, query_grad, preferred_element_type=jnp.float32
    )
    local_output = jnp.einsum("bte,btc->ec", out_all, out_grad, preferred_element_type=jnp.float32)
    query_weight_grad, output_weight_grad = lax.psum((local_query, local_output), "pb")
    return (hidden_grad, key_grad, value_grad, query_weight_grad, output_weight_grad)


def solution(mesh):
    in_specs = (
        P("pb", None, "psg"),
        P("pb", None, "psg"),
        P("psg", None),
        P(None, "psg"),
        P("pb", "psg", None),
        P("pb", "psg", None),
        P("pb", "psg", None),
        P("pb", "psg", None),
        P("pb", "psg", None, None),
        P("pb", "psg", None, None),
        P("pb", "psg"),
    )
    out_specs = (
        P("pb", None, "psg"),
        P("pb", "psg", None, None),
        P("pb", "psg", None, None),
        P("psg", None),
        P(None, "psg"),
    )
    return jax.shard_map(local, mesh=mesh, in_specs=in_specs, out_specs=out_specs, check_vma=False)
```

profile of v0, /device:TPU:1, one launch (start us, length us, event | category | flops | bytes accessed | tf_op | source)
XLA Modules:
  0.0 740.8 jit_solution(6140068273316505213)
XLA Ops:
  7.2 0.0 copy-start
  7.2 0.0 all-reduce.8.cloned.1.call-start
  7.3 6.2 copy.57
  13.4 3.2 reshape.121
  16.6 0.0 copy-start.1
  16.7 0.0 copy-done.12
  16.7 33.9 %all_gather.23 = f32[1,32,32]{2,0,1:T(1,128)S(1)} all-gather(f32[1,1,32]{2,0,1:T(1,128)S(1)} %bitcast.98), channel_id=1, replica_groups=mesh['psg'=32,'pb'=8] {'psg'}, dimensions={1}, use_global_device_ids=true | all-gather | bytes 4224 | tf_op jit(solution)/shard_map/all_gather | solution.py:42
  50.6 0.1 copy.62
  50.7 0.0 copy-done.13
  50.7 27.2 %all_gather.22 = f32[1,32,32]{2,0,1:T(1,128)S(1)} all-gather(f32[1,1,32]{2,0,1:T(1,128)S(1)} %bitcast.99), channel_id=1, replica_groups=mesh['psg'=32,'pb'=8] {'psg'}, dimensions={1}, use_global_device_ids=true | all-gather | bytes 4224 | tf_op jit(solution)/shard_map/all_gather | solution.py:41
  77.9 0.1 copy.60
  78.0 0.0 copy-done.10
  78.0 35.7 %all_gather.21 = bf16[1,32,2048]{2,0,1:T(2,128)(2,1)S(1)} all-gather(bf16[1,1,2048]{2,0,1:T(2,128)(2,1)S(1)} %bitcast.95), channel_id=1, replica_groups=mesh['psg'=32,'pb'=8] {'psg'}, dimensions={1}, use_global_device_ids=true | all-gather | bytes 135168 | tf_op jit(solution)/shard_map/all_gather | solution.py:37
  113.6 0.7 convert_reduce_fusion.1
  114.4 0.2 reshape.120
  114.6 6.1 copy.64
  120.8 4.4 reshape.124
  125.2 0.0 copy-done
  125.2 0.0 copy-done.7
  125.2 0.3 convolution_bitcast_fusion.1
  125.4 114.0 %all-reduce.9 = bf16[1,32,2048]{2,1,0:T(8,128)(2,1)S(1)} all-reduce(f32[1,32,2048]{2,1,0:T(8,128)S(1)} %convolution_bitcast_fusion.1), channel_id=3, replica_groups=mesh['psg'=32,'pb'=8] {'psg'}, use_global_device_ids=true, to_apply=%region_0.0.clone | all-reduce | flops 65536 | bytes 393216
  239.4 0.0 copy-done.11
  239.4 0.6 fusion.19
  240.0 0.7 fusion.18
  240.7 0.7 multiply_reduce_fusion
  241.4 0.1 reshape.125
  241.4 0.1 reduce_sum.11
  242.2 0.2 dynamic-update-slice
  242.5 55.7 %all-reduce = f32[1024]{0:T(1024)S(1)} all-reduce(f32[1024]{0:T(1024)S(1)} %dynamic-update-slice), channel_id=2, replica_groups=mesh['psg'=32,'pb'=8] {'psg'}, use_global_device_ids=true, to_apply=%add | all-reduce | flops 1024 | bytes 8192
  298.2 0.1 reshape.132
  298.3 0.1 copy.66
  298.3 36.4 %all_gather.24 = bf16[1,32,2048]{2,0,1:T(2,128)(2,1)S(1)} all-gather(bf16[1,1,2048]{2,0,1:T(2,128)(2,1)S(1)} %fusion.18), channel_id=1, replica_groups=mesh['psg'=32,'pb'=8] {'psg'}, dimensions={1}, use_global_device_ids=true | all-gather | bytes 135168 | tf_op jit(solution)/shard_map/all_gather | solution.py:39
  334.7 0.7 convert_reduce_fusion
  335.4 0.2 reshape.123
  335.7 0.0 copy-done.14
  335.7 0.1 lt.16
  335.8 0.0 copy-done.1
  335.8 0.0 copy-start.3
  335.8 0.7 select_divide_fusion
  336.5 0.8 copy-done.3
  337.4 0.5 multiply_convert_fusion
  337.9 0.8 copy-done.4
  338.7 1.0 copy-done.2
  339.7 0.7 convolution_bitcast_fusion.2
  340.4 0.3 copy.67
  340.7 0.2 reshape.126
  340.9 113.3 %all-reduce.10 = bf16[1,32,2048]{2,1,0:T(8,128)(2,1)S(1)} all-reduce(f32[1,32,2048]{2,1,0:T(8,128)S(1)} %reshape.126), channel_id=4, replica_groups=mesh['psg'=32,'pb'=8] {'psg'}, use_global_device_ids=true, to_apply=%region_2.3.clone | all-reduce | flops 65536 | bytes 393216
  454.3 0.7 fusion.13
  454.9 34.6 %all_gather.26 = bf16[1,32,2048]{2,0,1:T(2,128)(2,1)S(1)} all-gather(bf16[1,1,2048]{2,0,1:T(2,128)(2,1)S(1)} %fusion.13), channel_id=1, replica_groups=mesh['psg'=32,'pb'=8] {'psg'}, dimensions={1}, use_global_device_ids=true | all-gather | bytes 135168 | tf_op jit(solution)/shard_map/all_gather | solution.py:83
  489.5 37.6 %all_gather.27 = bf16[1,32,2048]{2,0,1:T(2,128)(2,1)S(1)} all-gather(bf16[1,1,2048]{2,0,1:T(2,128)(2,1)S(1)} %bitcast.94), channel_id=1, replica_groups=mesh['psg'=32,'pb'=8] {'psg'}, dimensions={1}, use_global_device_ids=true | all-gather | bytes 135168 | tf_op jit(solution)/shard_map/all_gather | solution.py:38
  527.1 1.3 fusion.7
  528.4 0.0 copy-done.9
  528.4 1.3 convolution_bitcast_fusion
  529.7 0.0 all-reduce.8.cloned.1.call-update
  529.7 2.1 convert_bitcast_fusion.1
  531.8 4.0 reshape.128
  535.8 6.3 copy.73
  542.1 2.1 convert_bitcast_fusion
  544.1 2.5 reshape.129
  546.7 4.6 copy.74
  551.3 1.9 fusion
  553.2 177.1 %all-reduce.8.cloned.1.call-done = (f32[128,2048]{0,1:T(8,128)}, f32[2048,128]{1,0:T(8,128)}) async-done(((f32[128,2048]{0,1:T(8,128)}, f32[2048,128]{1,0:T(8,128)}), (f32[128,2048]{0,1:T(8,128)}, f32[2048,128]{1,0:T(8,128)})) %all-reduce.8.cloned.1.call-update) | async-done | bytes 2097168 | tf_op jit(solution)/shard_map/psum | solution.py:91
  730.3 2.6 copy.75
  732.9 1.0 copy.109
  (19 shorter events, 0.0 us)
Async XLA Ops:
  7.2 118.0 %copy-start = (bf16[2048,128]{1,0:T(8,128)(2,1)S(1)}, bf16[2048,128]{1,0:T(8,128)(2,1)}, u32[]{:S(2)}) copy-start(bf16[2048,128]{1,0:T(8,128)(2,1)} %param.14) | copy-start | bytes 1572868
  7.2 723.1 %all-reduce.8.cloned.1.call-start = ((), (), s32[]{:S(2)}) async-start(), calls=%async_computation | async-start | bytes 4194304 | tf_op jit(solution)/shard_map/psum | solution.py:91
  13.4 3.2 copy-start.12
  13.4 37.2 %copy-start.13 = (f32[1,1,32]{2,1,0:T(1,128)S(1)}, f32[1,1,32]{2,1,0:T(1,128)}, u32[]{:S(2)}) copy-start(f32[1,1,32]{2,1,0:T(1,128)} %param.17) | copy-start | bytes 388
  13.4 64.5 %copy-start.10 = (bf16[1,1,2048]{2,1,0:T(2,128)(2,1)S(1)}, bf16[1,1,2048]{2,1,0:T(2,128)(2,1)}, u32[]{:S(2)}) copy-start(bf16[1,1,2048]{2,1,0:T(2,128)(2,1)} %param.15) | copy-start | bytes 12292
  16.6 319.1 %copy-start.1 = (bf16[512,32,64]{0,2,1:T(8,128)(2,1)}, bf16[512,32,64]{0,2,1:T(8,128)(2,1)S(1)}, u32[]{:S(2)}) copy-start(bf16[512,32,64]{0,2,1:T(8,128)(2,1)S(1)} %reshape.121) | copy-start | bytes 6291460
  120.8 4.4 copy-start.7
  120.8 118.7 %copy-start.11 = (u32[256]{0:T(256)S(1)}, u32[256]{0:T(256)}, u32[]{:S(2)}) copy-start(u32[256]{0:T(256)} %constant.13) | copy-start | bytes 3076
  120.8 119.9 %copy-start.8 = (bf16[1,1,2048]{2,1,0:T(2,128)(2,1)S(1)}, bf16[1,1,2048]{2,1,0:T(2,128)(2,1)}, u32[]{:S(2)}) copy-start(bf16[1,1,2048]{2,1,0:T(2,128)(2,1)} %param.16) | copy-start | bytes 12292
  125.2 210.5 %copy-start.14 = (s32[1,2]{1,0:T(1,128)S(1)}, s32[1,2]{1,0:T(1,128)}, u32[]{:S(2)}) copy-start(s32[1,2]{1,0:T(1,128)} %param.21) | copy-start | bytes 28
  335.8 1.6 copy-start.3
  337.4 1.4 copy-start.4
  337.4 2.3 copy-start.2
  340.4 188.0 %copy-start.9 = (bf16[1,32,128]{2,1,0:T(8,128)(2,1)S(1)}, bf16[1,32,128]{2,1,0:T(8,128)(2,1)}, u32[]{:S(2)}) copy-start(bf16[1,32,128]{2,1,0:T(8,128)(2,1)} %param.11) | copy-start | bytes 24580
  535.8 6.3 copy-start.5
  730.3 2.6 copy-start.6
Sparse Core Ops, SparseCore 0:
  529.8 200.4 all-reduce.7
where the time goes:
time: 743 us; the launch traced here: 741 us
  blocking collectives  488 us (66%)
  waiting for transfers between devices  177 us (24%)
  local copies, waits for them, and re-layouts  48.7 us (7%)
  between operations  14.9 us (2%)
  matrix products  10.9 us (1%)
    unnamed x3, blocking collectives  283 us
    psum x1, waiting for transfers between devices, local(): lax.psum((local_query, local_output), 'pb')  177 us
    all_gather x1, blocking collectives, local(): lax.all_gather(attn_out.astype(jnp.float32), 'psg', axis=1, tiled=True)  37.6 us
    all_gather x1, blocking collectives, local(): lax.all_gather(grad_rows.astype(jnp.float32), 'psg', axis=1, tiled=True)  36.4 us
    all_gather x1, blocking collectives, local(): lax.all_gather(queries.astype(jnp.float32), 'psg', axis=1, tiled=True)  35.7 us
    all_gather x1, blocking collectives, local(): query_grad = lax.all_gather(query_rows, 'psg', axis=1, tiled=True)  34.6 us
    all_gather x1, blocking collectives, local(): lax.all_gather(row_sum, 'psg', axis=1, tiled=True)  33.9 us
    unnamed x41, local copies, waits for them, and re-layouts  30.4 us
  transfers between devices with their start and end apart: 1, of which 1 were waited for; matrix products, arithmetic and copies ran while one was open for 3% of the time, Pallas kernels for 0%

commit v1 on v0

v1 whole, which is shorter than its diff:
```python
import functools

import jax
import jax.numpy as jnp
from jax import lax
from jax.experimental import pallas as pl
from jax.experimental.pallas import tpu as pltpu
from jax.sharding import PartitionSpec as P

MESH = pl.DeviceIdType.MESH
F32 = jnp.float32
BF16 = jnp.bfloat16

NT = (((1,), (1,)), ((), ()))
TN = (((0,), (0,)), ((), ()))
NN = (((1,), (0,)), ((), ()))

Z, Y, PSG, PB = 8, 4, 32, 8
GROUPS = 8


def dot(a, b, dims):
    return lax.dot_general(a, b, dims, preferred_element_type=F32)


def columns(pieces):
    left = jnp.concatenate([pieces[0], pieces[1]], axis=0)
    right = jnp.concatenate([pieces[2], pieces[3]], axis=0)
    return jnp.concatenate([left, right], axis=1)


def head_blocks(rows):
    tiled = jnp.concatenate([rows] * 4, axis=0)
    row = lax.broadcasted_iota(jnp.int32, tiled.shape, 0) // 32
    col = lax.broadcasted_iota(jnp.int32, tiled.shape, 1) // 64
    return jnp.where(row == col, tiled, jnp.zeros_like(tiled))


def far_first(n):
    kz, ky = n // 4, n % 4
    dz = 4 + (1 - 2 * (kz % 2)) * ((kz + 1) // 2)
    dy = 2 + (1 - 2 * (ky % 2)) * ((ky + 1) // 2)
    return dz, dy


def split_bf16(x, terms):
    out = []
    for _ in range(terms):
        part = x.astype(BF16)
        out.append(part)
        x = x - part.astype(F32)
    return out


def comm_kernel(
    dec_hbm, grad_hbm, weight_hbm, query_hbm, attn_hbm, max_hbm, sum_hbm, keys_hbm, values_hbm, len_hbm,
    probs_out, sgrad_out, q_out, g_out, qg_out, o_out, dg_out,
    weight, keys, values, query_ref, attn_ref, max_ref, sum_ref, len_ref, bundle, qa, qa32, stat_src, stats, partial, part_in, g_own, g_all, q_all,
    probs, probs_low, sgrad, qpart, qpart_in, qg_own, qg_all, o_all, dg_src, dg_all,
    local_sem, send_sem, recv_sem, x_send, x_recv, out_sem,
):
    me, pb = lax.axis_index("psg"), lax.axis_index("pb")
    z, y = me // Y, me % Y
    core, xpos = pb % 2, pb // 2
    slot = core * 4 + xpos
    partner = pb + 1 - 2 * core

    def psg_peer(n):
        dz, dy = far_first(n)
        return ((z + dz) % Z) * Y + (y + dy) % Y

    barrier = pltpu.get_barrier_semaphore()

    def greet(n, carry):
        pl.semaphore_signal(barrier, inc=1, device_id=(psg_peer(n), pb), device_id_type=MESH)
        return carry

    lax.fori_loop(0, PSG - 1, greet, 0)
    for d in range(1, PB):
        pl.semaphore_signal(barrier, inc=1, device_id=(me, (pb + d) % PB), device_id_type=MESH)

    loads = [
        pltpu.make_async_copy(src, dst, local_sem.at[i])
        for i, (src, dst) in enumerate((
            (query_hbm, query_ref), (attn_hbm, attn_ref), (max_hbm, max_ref), (sum_hbm, sum_ref),
            (dec_hbm, dg_src.at[0]), (grad_hbm, dg_src.at[1]), (weight_hbm, weight), (len_hbm, len_ref),
            (keys_hbm, keys), (values_hbm, values),
        ))
    ]
    for load in loads:
        load.start()
    keys_copy, values_copy = loads[8:]
    for load in loads[:6]:
        load.wait()

    for k in range(16):
        bundle[k : k + 1, :] = query_ref[:, k * 128 : (k + 1) * 128].astype(F32)
        bundle[16 + k : 17 + k, :] = attn_ref[:, k * 128 : (k + 1) * 128].astype(F32)
    qa_own = bundle[...].astype(BF16)
    qa[me] = qa_own
    stat_src[...] = jnp.zeros_like(stat_src)
    stat_src[0:1, 0:32] = max_ref[...] + jnp.log(sum_ref[...])
    stats[me] = stat_src[...]
    dg_all[slot] = dg_src[...]

    loads[6].wait()
    loads[7].wait()
    grad = dg_src[1]
    for k in range(16):
        block = dot(grad, weight[k * 128 : (k + 1) * 128, :], NT).astype(BF16)
        partial[2 * k] = block[0:16]
        partial[2 * k + 1] = block[16:32]

    pl.semaphore_wait(barrier, PSG - 1 + PB - 1)

    def scatter(src, dst, i):
        def go(n, carry):
            to = psg_peer(n)
            pltpu.make_async_remote_copy(
                src_ref=src.at[to], dst_ref=dst.at[me], send_sem=send_sem.at[i], recv_sem=recv_sem.at[i],
                device_id=(to, pb), device_id_type=MESH,
            ).start()
            return carry

        lax.fori_loop(0, PSG - 1, go, 0)

    def broadcast(src, dst, i):
        def go(n, carry):
            pltpu.make_async_remote_copy(
                src_ref=src, dst_ref=dst, send_sem=send_sem.at[i], recv_sem=recv_sem.at[i],
                device_id=(psg_peer(n), pb), device_id_type=MESH,
            ).start()
            return carry

        lax.fori_loop(0, PSG - 1, go, 0)

    def wait_bytes(ref, sem):
        pltpu.make_async_copy(ref, ref, sem).wait()

    scatter(partial, part_in, 0)
    part_in[me] = partial[me]
    broadcast(qa.at[me], qa.at[me], 1)
    broadcast(stats.at[me], stats.at[me], 2)
    for d in range(1, PB):
        pltpu.make_async_remote_copy(
            src_ref=dg_src, dst_ref=dg_all.at[slot], send_sem=x_send.at[14], recv_sem=x_recv.at[14],
            device_id=(me, (pb + d) % PB), device_id_type=MESH,
        ).start()

    def x_start(buf, base):
        for d in range(1, 4):
            pltpu.make_async_remote_copy(
                src_ref=buf.at[slot], dst_ref=buf.at[slot], send_sem=x_send.at[base + d], recv_sem=x_recv.at[base + d],
                device_id=(me, (pb + 2 * d) % PB), device_id_type=MESH,
            ).start()
        pltpu.make_async_remote_copy(
            src_ref=buf.at[slot], dst_ref=buf.at[slot], send_sem=x_send.at[base], recv_sem=x_recv.at[base],
            device_id=(me, partner), device_id_type=MESH,
        ).start()

    def x_forward(buf, base):
        for d in (1, 3, 2):
            wait_bytes(buf.at[0], x_recv.at[base + d])
            got = core * 4 + (xpos + 4 - d) % 4
            pltpu.make_async_remote_copy(
                src_ref=buf.at[got], dst_ref=buf.at[got], send_sem=x_send.at[base + 3 + d], recv_sem=x_recv.at[base + 3 + d],
                device_id=(me, partner), device_id_type=MESH,
            ).start()

    def x_finish(buf, base):
        for k in (0, 4, 6, 5):
            wait_bytes(buf.at[0], x_recv.at[base + k])

    def x_drain(buf, base):
        for k in range(7):
            wait_bytes(buf.at[0], x_send.at[base + k])

    wait_bytes(part_in.at[pl.ds(0, PSG - 1)], recv_sem.at[0])
    g_own[...] = jnp.sum(part_in[...].astype(F32), axis=0).astype(BF16)
    broadcast(g_own, g_all.at[me], 3)
    g_all[me] = g_own[...]

    wait_bytes(qa.at[pl.ds(0, PSG - 1)], recv_sem.at[1])
    qa32[...] = qa[...].astype(F32)
    for k in range(16):
        block = qa32[:, k, :].astype(BF16)
        q_all[2 * k] = block[0:16]
        q_all[2 * k + 1] = block[16:32]
        block = qa32[:, 16 + k, :].astype(BF16)
        o_all[slot, 2 * k] = block[0:16]
        o_all[slot, 2 * k + 1] = block[16:32]
    x_start(o_all, 0)
    q_copy = pltpu.make_async_copy(q_all, q_out, out_sem.at[0])
    q_copy.start()

    wait_bytes(stats.at[pl.ds(0, PSG - 1)], recv_sem.at[2])
    stat_rows = jnp.concatenate([stats[t, 0:1, :] for t in range(PSG)], axis=0)
    head = lax.broadcasted_iota(jnp.int32, (128, 1024), 0)
    lane = lax.broadcasted_iota(jnp.int32, (128, 1024), 1)
    pick = jnp.where(head == lane // 32, 1.0, 0.0).astype(BF16)
    spread = sum(dot(part, pick, NN) for part in split_bf16(stat_rows, 3))
    token = lax.broadcasted_iota(jnp.int32, (32, 1024), 0)
    lane = lax.broadcasted_iota(jnp.int32, (32, 1024), 1)
    stat_lanes = jnp.sum(jnp.where(token == lane % 32, spread, 0.0), axis=0, keepdims=True)

    keys_copy.wait()
    position = lax.broadcasted_iota(jnp.int32, (256, 128), 0)
    for g in range(GROUPS):
        wide, narrow = pl.ds(g * 256, 256), pl.ds(g * 128, 128)
        blocks = head_blocks(columns(q_all[pl.ds(g * 4, 4)]))
        scores = dot(keys[:, wide], blocks, NT) - stat_lanes[:, g * 128 : (g + 1) * 128]
        for p in range(2):
            rows = pl.ds(p * 256, 256)
            value = jnp.where(position < len_ref[0, p], jnp.exp(scores[p * 256 : (p + 1) * 256]), 0.0)
            probs[rows, narrow] = value
            probs_low[rows, narrow] = value.astype(BF16)
    probs_copy = pltpu.make_async_copy(probs_low, probs_out, out_sem.at[1])
    probs_copy.start()

    wait_bytes(g_all.at[pl.ds(0, PSG - 1)], recv_sem.at[3])
    g_copy = pltpu.make_async_copy(g_all, g_out, out_sem.at[2])
    g_copy.start()
    values_copy.wait()
    ones = jnp.ones((8, 256), BF16)
    for g in range(GROUPS):
        wide, narrow = pl.ds(g * 256, 256), pl.ds(g * 128, 128)
        blocks = head_blocks(columns(g_all[pl.ds(g * 4, 4)]))
        out_rows = columns(o_all[slot, pl.ds(g * 4, 4)]).astype(F32)
        product = blocks.astype(F32) * jnp.concatenate([out_rows] * 4, axis=0)
        delta = sum(dot(ones, part, NT) for part in split_bf16(product, 3))[0:1]
        prob_grad = dot(values[:, wide], blocks, NT)
        score_grad = (probs[:, narrow] * (prob_grad - delta)).astype(BF16)
        sgrad[:, narrow] = score_grad
        part = dot(score_grad, keys[:, wide], TN)
        head = lax.broadcasted_iota(jnp.int32, part.shape, 0) // 32
        col = lax.broadcasted_iota(jnp.int32, part.shape, 1) // 64
        part = jnp.where(head == col, part, 0.0)
        part = (part[0:32] + part[32:64] + part[64:96] + part[96:128]).astype(BF16)
        qpart[4 * g] = part[0:16, 0:128]
        qpart[4 * g + 1] = part[16:32, 0:128]
        qpart[4 * g + 2] = part[0:16, 128:256]
        qpart[4 * g + 3] = part[16:32, 128:256]
    scatter(qpart, qpart_in, 4)
    qpart_in[me] = qpart[me]
    sgrad_copy = pltpu.make_async_copy(sgrad, sgrad_out, out_sem.at[3])
    sgrad_copy.start()

    x_forward(o_all, 0)

    wait_bytes(qpart_in.at[pl.ds(0, PSG - 1)], recv_sem.at[4])
    qg_own[...] = jnp.sum(qpart_in[...].astype(F32), axis=0).astype(BF16)
    broadcast(qg_own, qg_all.at[slot, me], 5)
    qg_all[slot, me] = qg_own[...]

    wait_bytes(dg_all.at[pl.ds(0, PB - 1)], x_recv.at[14])
    dg_copy = pltpu.make_async_copy(dg_all, dg_out, out_sem.at[4])
    dg_copy.start()
    x_finish(o_all, 0)
    o_copy = pltpu.make_async_copy(o_all, o_out, out_sem.at[5])
    o_copy.start()

    wait_bytes(qg_all.at[slot, pl.ds(0, PSG - 1)], recv_sem.at[5])
    x_start(qg_all, 7)
    x_forward(qg_all, 7)
    x_finish(qg_all, 7)
    qg_copy = pltpu.make_async_copy(qg_all, qg_out, out_sem.at[6])
    qg_copy.start()

    wait_bytes(partial.at[pl.ds(0, PSG - 1)], send_sem.at[0])
    wait_bytes(qa.at[pl.ds(0, PSG - 1)], send_sem.at[1])
    wait_bytes(stats.at[pl.ds(0, PSG - 1)], send_sem.at[2])
    wait_bytes(g_all.at[pl.ds(0, PSG - 1)], send_sem.at[3])
    wait_bytes(qpart.at[pl.ds(0, PSG - 1)], send_sem.at[4])
    wait_bytes(qpart.at[pl.ds(0, PSG - 1)], send_sem.at[5])
    wait_bytes(dg_all.at[pl.ds(0, PB - 1)], x_send.at[14])
    x_drain(o_all, 0)
    x_drain(qg_all, 7)
    for copy in (q_copy, probs_copy, g_copy, sgrad_copy, dg_copy, o_copy, qg_copy):
        copy.wait()


def grads_kernel(
    probs_ref, sgrad_ref, q_ref, g_ref, qg_ref, o_ref, dg_ref, qw_ref,
    hidden_ref, kgrad_ref, vgrad_ref, qwg_ref, owg_ref, acc,
):
    g = pl.program_id(0)
    pb = lax.axis_index("pb")
    slot = (pb % 2) * 4 + pb // 2
    vgrad_ref[...] = dot(probs_ref[...], head_blocks(columns(g_ref[...])), NN).astype(BF16)
    kgrad_ref[...] = dot(sgrad_ref[...], head_blocks(columns(q_ref[...])), NN).astype(BF16)

    def all_questions(ref):
        return jnp.concatenate([columns(ref[s]) for s in range(PB)], axis=0)

    tokens = jnp.concatenate([dg_ref[s, 0] for s in range(PB)], axis=0)
    qwg_ref[...] = dot(tokens, all_questions(qg_ref), TN)
    tokens = jnp.concatenate([dg_ref[s, 1] for s in range(PB)], axis=0)
    owg_ref[...] = dot(all_questions(o_ref), tokens, TN)
    part = dot(columns(qg_ref[slot]), qw_ref[...], NT)

    @pl.when(g == 0)
    def _():
        acc[...] = part

    @pl.when(g > 0)
    def _():
        acc[...] += part

    @pl.when(g == GROUPS - 1)
    def _():
        hidden_ref[...] = acc[...].astype(BF16)


def local(
    dec_hidden, out_grad, query_weight, output_weight, queries, attn_out, row_max, row_sum, keys, values, lengths
):
    hbm = pl.BlockSpec(memory_space=pl.ANY)
    sds = jax.ShapeDtypeStruct
    pieces = (PSG, 16, 128)
    probs, sgrad, q_all, g_all, qg_all, o_all, dg_all = pl.pallas_call(
        comm_kernel,
        out_shape=[
            sds((512, 1024), BF16), sds((512, 1024), BF16), sds(pieces, BF16), sds(pieces, BF16),
            sds((PB,) + pieces, BF16), sds((PB,) + pieces, BF16), sds((PB, 2, 32, 128), BF16),
        ],
        in_specs=[hbm] * 10,
        out_specs=[hbm] * 7,
        scratch_shapes=[
            pltpu.VMEM((2048, 128), BF16),
            pltpu.VMEM((512, 2048), BF16),
            pltpu.VMEM((512, 2048), BF16),
            pltpu.VMEM((1, 2048), BF16),
            pltpu.VMEM((1, 2048), BF16),
            pltpu.VMEM((1, 32), F32),
            pltpu.VMEM((1, 32), F32),
            pltpu.SMEM((1, 2), jnp.int32),
            pltpu.VMEM((32, 128), F32),
            pltpu.VMEM((PSG, 32, 128), BF16),
            pltpu.VMEM((PSG, 32, 128), F32),
            pltpu.VMEM((8, 128), F32),
            pltpu.VMEM((PSG, 8, 128), F32),
            pltpu.VMEM(pieces, BF16),
            pltpu.VMEM(pieces, BF16),
            pltpu.VMEM((16, 128), BF16),
            pltpu.VMEM(pieces, BF16),
            pltpu.VMEM(pieces, BF16),
            pltpu.VMEM((512, 1024), F32),
            pltpu.VMEM((512, 1024), BF16),
            pltpu.VMEM((512, 1024), BF16),
            pltpu.VMEM(pieces, BF16),
            pltpu.VMEM(pieces, BF16),
            pltpu.VMEM((16, 128), BF16),
            pltpu.VMEM((PB,) + pieces, BF16),
            pltpu.VMEM((PB,) + pieces, BF16),
            pltpu.VMEM((2, 32, 128), BF16),
            pltpu.VMEM((PB, 2, 32, 128), BF16),
            pltpu.SemaphoreType.DMA((10,)),
            pltpu.SemaphoreType.DMA((6,)),
            pltpu.SemaphoreType.DMA((6,)),
            pltpu.SemaphoreType.DMA((15,)),
            pltpu.SemaphoreType.DMA((15,)),
            pltpu.SemaphoreType.DMA((7,)),
        ],
        compiler_params=pltpu.CompilerParams(collective_id=1, has_side_effects=True, vmem_limit_bytes=62 * 2**20),
        cost_estimate=pl.CostEstimate(flops=10**9, bytes_accessed=10**7, transcendentals=512 * 1024),
        name="comm",
    )(
        dec_hidden.reshape(32, 128), out_grad.reshape(32, 128), output_weight,
        queries.reshape(1, 2048), attn_out.reshape(1, 2048), row_max.reshape(1, 32), row_sum.reshape(1, 32),
        keys.reshape(512, 2048), values.reshape(512, 2048), lengths,
    )

    def whole(shape):
        return pl.BlockSpec(shape, lambda g: (0,) * len(shape))

    hidden, kgrad, vgrad, qwg, owg = pl.pallas_call(
        grads_kernel,
        grid=(GROUPS,),
        out_shape=[
            sds((32, 128), BF16), sds((512, 2048), BF16), sds((512, 2048), BF16),
            sds((128, 2048), F32), sds((2048, 128), F32),
        ],
        in_specs=[
            pl.BlockSpec((512, 128), lambda g: (0, g)), pl.BlockSpec((512, 128), lambda g: (0, g)),
            pl.BlockSpec((4, 16, 128), lambda g: (g, 0, 0)), pl.BlockSpec((4, 16, 128), lambda g: (g, 0, 0)),
            pl.BlockSpec((PB, 4, 16, 128), lambda g: (0, g, 0, 0)), pl.BlockSpec((PB, 4, 16, 128), lambda g: (0, g, 0, 0)),
            whole((PB, 2, 32, 128)),
            pl.BlockSpec((128, 256), lambda g: (0, g)),
        ],
        out_specs=[
            whole((32, 128)), pl.BlockSpec((512, 256), lambda g: (0, g)), pl.BlockSpec((512, 256), lambda g: (0, g)),
            pl.BlockSpec((128, 256), lambda g: (0, g)), pl.BlockSpec((256, 128), lambda g: (g, 0)),
        ],
        scratch_shapes=[pltpu.VMEM((32, 128), F32)],
        compiler_params=pltpu.CompilerParams(vmem_limit_bytes=62 * 2**20),
        cost_estimate=pl.CostEstimate(flops=10**9, bytes_accessed=10**7, transcendentals=0),
        name="grads",
    )(probs, sgrad, q_all, g_all, qg_all, o_all, dg_all, query_weight)
    return (
        hidden.reshape(dec_hidden.shape), kgrad.reshape(keys.shape), vgrad.reshape(values.shape), qwg, owg
    )


def solution(mesh):
    in_specs = (
        P("pb", None, "psg"),
        P("pb", None, "psg"),
        P("psg", None),
        P(None, "psg"),
        P("pb", "psg", None),
        P("pb", "psg", None),
        P("pb", "psg", None),
        P("pb", "psg", None),
        P("pb", "psg", None, None),
        P("pb", "psg", None, None),
        P("pb", "psg"),
    )
    out_specs = (
        P("pb", None, "psg"),
        P("pb", "psg", None, None),
        P("pb", "psg", None, None),
        P("psg", None),
        P(None, "psg"),
    )
    return jax.shard_map(local, mesh=mesh, in_specs=in_specs, out_specs=out_specs, check_vma=False)
```

time: 743 us -> 62.2 us (0.08)
  blocking collectives: 488 us -> 0 us
  waiting for transfers between devices: 177 us -> 0 us
  Pallas kernels: 0 us -> 61.3 us
  local copies, waits for them, and re-layouts: 48.7 us -> 0 us
  between operations: 14.9 us -> 0.64 us
  matrix products: 10.9 us -> 0 us
    unnamed x3 -> x0, blocking collectives: 283 us -> none
    all_gather x6 -> x0, blocking collectives: 205 us -> none  [the longest x1 37.6 us: local(): lax.all_gather(attn_out.astype(jnp.float32), 'psg', axis=1, tiled=True)]
    psum x1 -> x0, waiting for transfers between devices: 177 us -> none  [local(): lax.psum((local_query, local_output), 'pb')]
    pallas_call x0 -> x2, Pallas kernels: none -> 61.3 us  [the longest x1 52.1 us: local(): pl.pallas_call(comm_kernel, out_shape=[sds((512, 1024), BF16), sds((512,...]
    unnamed x41 -> x0, local copies, waits for them, and re-layouts: 30.4 us -> none
    dot_general x9 -> x0, matrix products: 10.9 us -> none  [the longest x1 2.08 us: local(): jnp.einsum('bhts,bthd->bshd', score_grad, query_heads, preferred_element_...]
    another operation x4 -> x0, local copies, waits for them, and re-layouts: 8.08 us -> none
  transfers between devices with their start and end apart: 1 -> 0, of which waited for: 1 -> 0; matrix products, arithmetic and copies ran while one was open for 3% -> 0% of each run, Pallas kernels for 0% -> 0%
where the time goes in v1:
time: 62.2 us; the launch traced here: 62 us
  Pallas kernels  61.3 us (99%)
  between operations  0.64 us (1%)
    pallas_call x1, Pallas kernels, local(): pl.pallas_call(comm_kernel, out_shape=[sds((512, 1024), BF16), sds((512,...  52.1 us
    pallas_call x1, Pallas kernels, local(): pl.pallas_call(grads_kernel, grid=(GROUPS,), out_shape=[sds((32, 128), BF...  9.23 us

profile of v1, /device:TPU:1, one launch (start us, length us, event | category | flops | bytes accessed | tf_op | source)
XLA Modules:
  0.0 62.0 jit_solution(13358259684070869244)
XLA Ops:
  0.6 52.1 %comm.1 = (bf16[512,1024]{1,0:T(8,128)(2,1)}, bf16[512,1024]{1,0:T(8,128)(2,1)}, bf16[32,16,128]{2,1,0:T(8,128)(2,1)}, bf16[32,16,128]{2,1,0:T(8,128)(2,1)}, bf1...) custom-call(bf16[32,128]{1,0:T(8,128)(2,1)} %bitcast.13, ...), custom_call_target="tpu_custom_call" | custom-call | flops 1000000000 | bytes 10000000 | tf_op jit(solution)/shard_map/comm/pallas_call | solution.py:320
  52.7 9.2 %grads.1 = (bf16[32,128]{1,0:T(8,128)(2,1)}, bf16[512,2048]{1,0:T(8,128)(2,1)}, bf16[512,2048]{1,0:T(8,128)(2,1)}, f32[128,2048]{1,0:T(8,128)}, f32[2048,128]{1,0:T(8,128)}) custom-call(bf16[512,1024]{1,0:T(8,128)(2,1)} %get-tuple-element.17.probs_ref, bf16[512,1024]{1,0:T(8,128)(2,1)} %get-tuple-element.18.sgrad_ref, ...), custom_call_target="tpu_custom_call" | custom-call | flops 1000000000 | bytes 10000000 | tf_op jit(solution)/shard_map/grads/pallas_call | solution.py:376

commit v2 on v1

v2 whole, which is shorter than its diff:
```python
import jax
import jax.numpy as jnp
from jax import lax
from jax.experimental import pallas as pl
from jax.experimental.pallas import tpu as pltpu
from jax.sharding import PartitionSpec as P

MESH = pl.DeviceIdType.MESH
F32 = jnp.float32
BF16 = jnp.bfloat16

NT = (((1,), (1,)), ((), ()))
TN = (((0,), (0,)), ((), ()))
NN = (((1,), (0,)), ((), ()))

Z, Y, PSG, PB = 8, 4, 32, 8
GROUPS = 8
NEAR = (0, 1, 7, 2, 6, 3, 5, 4)


def dot(a, b, dims):
    return lax.dot_general(a, b, dims, preferred_element_type=F32)


def columns(pieces):
    left = jnp.concatenate([pieces[0], pieces[1]], axis=0)
    right = jnp.concatenate([pieces[2], pieces[3]], axis=0)
    return jnp.concatenate([left, right], axis=1)


def head_blocks(rows):
    tiled = jnp.concatenate([rows] * 4, axis=0)
    row = lax.broadcasted_iota(jnp.int32, tiled.shape, 0) // 32
    col = lax.broadcasted_iota(jnp.int32, tiled.shape, 1) // 64
    return jnp.where(row == col, tiled, jnp.zeros_like(tiled))


def split_bf16(x, terms):
    out = []
    for _ in range(terms):
        part = x.astype(BF16)
        out.append(part)
        x = x - part.astype(F32)
    return out


def comm_kernel(
    dec_hbm, grad_hbm, weight_hbm, query_hbm, attn_hbm, max_hbm, sum_hbm, keys_hbm, values_hbm, len_hbm,
    probs_out, sgrad_out, q_out, g_out, qg_out, o_out, dg_out,
    weight, keys, values, query_ref, attn_ref, max_ref, sum_ref, len_ref, bundle, qa, qa32, stat_src, stats,
    partial, part_in, g_own, g_all, q_all, probs, probs_low, sgrad, qpart, qpart_in, qg_own, qg_all,
    o_all, dg_src, dg_all,
    local_sem, send_sem, recv_sem, x_send, x_recv, side_send, side_recv, core_send,
    core_recv, out_sem, qg_sem,
):
    me, pb = lax.axis_index("psg"), lax.axis_index("pb")
    z, y = lax.div(me, Y), lax.rem(me, Y)
    core, xpos = lax.rem(pb, 2), lax.div(pb, 2)
    slot = core * 4 + xpos
    partner = pb + 1 - 2 * core
    zs = [lax.rem(z + d, Z) for d in range(Z)]
    ys = [lax.rem(y + d, Y) for d in range(Y)]
    peers = {(dz, dy): zs[dz] * Y + ys[dy] for dz in range(Z) for dy in range(Y) if dz or dy}
    far_first = [peers[dz, dy] for dz in reversed(NEAR) for dy in (2, 1, 3, 0) if dz or dy]
    pb_peers = [lax.rem(pb + d, PB) for d in range(PB)]

    barrier = pltpu.get_barrier_semaphore()
    for to in far_first:
        pl.semaphore_signal(barrier, inc=1, device_id=(to, pb), device_id_type=MESH)
    for d in range(1, PB):
        pl.semaphore_signal(barrier, inc=1, device_id=(me, pb_peers[d]), device_id_type=MESH)

    loads = [
        pltpu.make_async_copy(src, dst, local_sem.at[i])
        for i, (src, dst) in enumerate((
            (query_hbm, query_ref), (attn_hbm, attn_ref), (max_hbm, max_ref), (sum_hbm, sum_ref),
            (dec_hbm, dg_src.at[0]), (grad_hbm, dg_src.at[1]), (weight_hbm, weight), (len_hbm, len_ref),
            (keys_hbm, keys), (values_hbm, values),
        ))
    ]
    for load in loads:
        load.start()
    keys_copy, values_copy = loads[8:]
    for load in loads[:6]:
        load.wait()

    for k in range(16):
        bundle[k : k + 1, :] = query_ref[:, k * 128 : (k + 1) * 128].astype(F32)
        bundle[16 + k : 17 + k, :] = attn_ref[:, k * 128 : (k + 1) * 128].astype(F32)
    qa[me] = bundle[...].astype(BF16)
    stat_src[...] = jnp.zeros_like(stat_src)
    stat_src[0:1, 0:32] = max_ref[...] + jnp.log(sum_ref[...])
    stats[me] = stat_src[...]
    dg_all[slot] = dg_src[...]

    loads[6].wait()
    loads[7].wait()
    grad = dg_src[1]
    for k in range(16):
        block = dot(grad, weight[k * 128 : (k + 1) * 128, :], NT).astype(BF16)
        partial[2 * k] = block[0:16]
        partial[2 * k + 1] = block[16:32]

    pl.semaphore_wait(barrier, PSG - 1 + PB - 1)

    def send(src, dst, send_at, recv_at, to):
        pltpu.make_async_remote_copy(
            src_ref=src, dst_ref=dst, send_sem=send_at, recv_sem=recv_at, device_id=to, device_id_type=MESH
        ).start()

    def wait_bytes(ref, sem):
        pltpu.make_async_copy(ref, ref, sem).wait()

    for dy in (2, 1, 3):
        send(stats.at[me], stats.at[me], send_sem.at[2], recv_sem.at[2], (peers[0, dy], pb))
    for to in far_first:
        send(partial.at[to], part_in.at[me], send_sem.at[0], recv_sem.at[0], (to, pb))
    part_in[me] = partial[me]
    for to in far_first:
        send(qa.at[me], qa.at[me], send_sem.at[1], recv_sem.at[1], (to, pb))
    row_of_four = pl.ds(z * Y, Y)
    wait_bytes(stats.at[pl.ds(0, Y - 1)], recv_sem.at[2])
    for dz in (4, 5, 3, 6, 2, 7, 1):
        send(stats.at[row_of_four], stats.at[row_of_four], send_sem.at[7], recv_sem.at[5], (peers[dz, 0], pb))

    wait_bytes(part_in.at[pl.ds(0, PSG - 1)], recv_sem.at[0])
    g_own[...] = jnp.sum(part_in[...].astype(F32), axis=0).astype(BF16)
    for to in far_first:
        send(g_own, g_all.at[me], send_sem.at[3], recv_sem.at[3], (to, pb))
    g_all[me] = g_own[...]
    for d in range(1, PB):
        send(dg_src, dg_all.at[slot], x_send.at[7], x_recv.at[7], (me, pb_peers[d]))

    wait_bytes(qa.at[pl.ds(0, PSG - 1)], recv_sem.at[1])
    qa32[...] = qa[...].astype(F32)
    for k in range(16):
        block = qa32[:, k, :].astype(BF16)
        q_all[2 * k] = block[0:16]
        q_all[2 * k + 1] = block[16:32]
        block = qa32[:, 16 + k, :].astype(BF16)
        o_all[slot, 2 * k] = block[0:16]
        o_all[slot, 2 * k + 1] = block[16:32]
    own = o_all.at[slot]
    for d in range(1, 4):
        send(own, own, x_send.at[d], x_recv.at[d], (me, pb_peers[2 * d]))
    send(own, own, x_send.at[0], x_recv.at[0], (me, partner))
    q_copy = pltpu.make_async_copy(q_all, q_out, out_sem.at[0])
    q_copy.start()

    wait_bytes(stats.at[pl.ds(0, PSG - Y)], recv_sem.at[5])
    stat_rows = jnp.concatenate([stats[t] for t in range(PSG)], axis=0)
    head = lax.broadcasted_iota(jnp.int32, (128, 1024), 0)
    lane = lax.broadcasted_iota(jnp.int32, (128, 1024), 1)
    pick = jnp.where(head == lane // 32, 1.0, 0.0).astype(BF16)
    spread = sum(dot(part, pick, NN) for part in split_bf16(stat_rows, 3))
    token = lax.broadcasted_iota(jnp.int32, (32, 1024), 0)
    lane = lax.broadcasted_iota(jnp.int32, (32, 1024), 1)
    stat_lanes = jnp.sum(jnp.where(token == lane % 32, spread, 0.0), axis=0, keepdims=True)

    keys_copy.wait()
    position = lax.broadcasted_iota(jnp.int32, (256, 128), 0)
    for g in range(GROUPS):
        blocks = head_blocks(columns(q_all[pl.ds(g * 4, 4)]))
        scores = dot(keys[:, g * 256 : (g + 1) * 256], blocks, NT) - stat_lanes[:, g * 128 : (g + 1) * 128]
        for p in range(2):
            rows = pl.ds(p * 256, 256)
            value = jnp.where(position < len_ref[0, p], jnp.exp(scores[p * 256 : (p + 1) * 256]), 0.0)
            probs[g, rows] = value
            probs_low[g, rows] = value.astype(BF16)
    probs_copy = pltpu.make_async_copy(probs_low, probs_out, out_sem.at[1])
    probs_copy.start()
    values_copy.wait()

    wait_bytes(g_all.at[pl.ds(0, PSG - 1)], recv_sem.at[3])
    ones = jnp.ones((8, 256), BF16)
    for g in range(GROUPS):
        four = pl.ds(g * 4, 4)
        blocks = head_blocks(columns(g_all[four]))
        out_rows = columns(o_all[slot, four]).astype(F32)
        product = blocks.astype(F32) * jnp.concatenate([out_rows] * 4, axis=0)
        delta = sum(dot(ones, part, NT) for part in split_bf16(product, 2))[0:1]
        prob_grad = dot(values[:, g * 256 : (g + 1) * 256], blocks, NT)
        sgrad[g] = (probs[g] * (prob_grad - delta)).astype(BF16)
    row = lax.broadcasted_iota(jnp.int32, (128, 256), 0) // 32
    col = lax.broadcasted_iota(jnp.int32, (128, 256), 1) // 64
    for g in range(GROUPS):
        part = jnp.where(row == col, dot(sgrad[g], keys[:, g * 256 : (g + 1) * 256], TN), 0.0)
        part = (part[0:32] + part[32:64] + part[64:96] + part[96:128]).astype(BF16)
        qpart[g * 4] = part[0:16, 0:128]
        qpart[g * 4 + 1] = part[16:32, 0:128]
        qpart[g * 4 + 2] = part[0:16, 128:256]
        qpart[g * 4 + 3] = part[16:32, 128:256]
    for to in far_first:
        send(qpart.at[to], qpart_in.at[me], send_sem.at[4], recv_sem.at[4], (to, pb))
    qpart_in[me] = qpart[me]
    g_copy = pltpu.make_async_copy(g_all, g_out, out_sem.at[2])
    g_copy.start()
    sgrad_copy = pltpu.make_async_copy(sgrad, sgrad_out, out_sem.at[3])
    sgrad_copy.start()

    for d in (1, 3, 2):
        wait_bytes(own, x_recv.at[d])
        got = o_all.at[core * 4 + lax.rem(xpos + 4 - d, 4)]
        send(got, got, x_send.at[3 + d], x_recv.at[3 + d], (me, partner))
    wait_bytes(dg_all.at[pl.ds(0, PB - 1)], x_recv.at[7])
    dg_copy = pltpu.make_async_copy(dg_all, dg_out, out_sem.at[4])
    dg_copy.start()

    wait_bytes(qpart_in.at[pl.ds(0, PSG - 1)], recv_sem.at[4])
    qg_own[...] = jnp.sum(qpart_in[...].astype(F32), axis=0).astype(BF16)
    opposite = core * 4 + lax.rem(xpos + 2, 4)
    send(qg_own, qg_all.at[slot, me], side_send.at[0], side_recv.at[0], (me, pb_peers[4]))
    for to in far_first:
        send(qg_own, qg_all.at[slot, me], send_sem.at[5], recv_sem.at[7], (to, pb))
    qg_all[slot, me] = qg_own[...]
    wait_bytes(qg_own, side_recv.at[0])
    for to in far_first:
        send(qg_all.at[opposite, me], qg_all.at[opposite, me], send_sem.at[6], recv_sem.at[8], (to, pb))

    for k in (0, 4, 6, 5):
        wait_bytes(own, x_recv.at[k])
    o_copy = pltpu.make_async_copy(o_all, o_out, out_sem.at[5])
    o_copy.start()
    copies = []

    for i, count, ref in (
        (0, PSG - 1, partial), (1, PSG - 1, qa), (2, Y - 1, stats), (3, PSG - 1, g_all), (4, PSG - 1, qpart),
        (5, PSG - 1, qpart), (7, PSG - Y, stats),
    ):
        wait_bytes(ref.at[pl.ds(0, count)], send_sem.at[i])
    for k in range(7):
        wait_bytes(own, x_send.at[k])
    wait_bytes(dg_all.at[pl.ds(0, PB - 1)], x_send.at[7])
    wait_bytes(qg_own, side_send.at[0])
    for copy in (q_copy, probs_copy, g_copy, sgrad_copy, dg_copy, o_copy):
        copy.wait()

    def keep(at, first, count):
        part = pl.ds(first, count)
        copies.append(pltpu.make_async_copy(qg_all.at[at, part], qg_out.at[at, part], qg_sem.at[len(copies)]))
        copies[-1].start()

    def hand_over(at, first, count, k):
        part = qg_all.at[at, pl.ds(first, count)]
        send(part, part, core_send.at[k], core_recv.at[k], (me, partner))

    wait_bytes(qg_all.at[slot, pl.ds(0, PSG - 1)], recv_sem.at[7])
    for half in range(2):
        part = qg_all.at[slot, pl.ds(16 * half, 16)]
        for i, d in enumerate((2, 6)):
            send(part, part, side_send.at[1 + 2 * half + i], side_recv.at[1 + 2 * half + i], (me, pb_peers[d]))
    hand_over(slot, 0, PSG, 0)
    keep(slot, 0, PSG)
    wait_bytes(qg_all.at[slot, pl.ds(0, PSG - 1)], recv_sem.at[8])
    hand_over(opposite, 0, PSG, 1)
    keep(opposite, 0, PSG)
    sides = [core * 4 + lax.rem(xpos + d, 4) for d in (3, 1)]
    for half in range(2):
        for i in range(2):
            wait_bytes(qg_all.at[slot, pl.ds(0, 16)], side_recv.at[1 + 2 * half + i])
            hand_over(sides[i], 16 * half, 16, 2 + 2 * half + i)
    for i in range(2):
        keep(sides[i], 0, PSG)
    for k, d in enumerate((0, 2)):
        wait_bytes(qg_all.at[slot], core_recv.at[k])
        keep(lax.rem(slot + 4, PB) if d == 0 else lax.rem(opposite + 4, PB), 0, PSG)
    for half in range(2):
        for i in range(2):
            wait_bytes(qg_all.at[slot, pl.ds(0, 16)], core_recv.at[2 + 2 * half + i])
            keep(lax.rem(sides[i] + 4, PB), 16 * half, 16)

    wait_bytes(qpart.at[pl.ds(0, PSG - 1)], send_sem.at[6])
    for k in range(1, 5):
        wait_bytes(qg_all.at[slot, pl.ds(0, 16)], side_send.at[k])
    for k in range(6):
        wait_bytes(qg_all.at[slot, pl.ds(0, PSG if k < 2 else 16)], core_send.at[k])
    for copy in copies:
        copy.wait()


def grads_kernel(
    probs_hbm, sgrad_hbm, q_hbm, g_hbm, qg_hbm, o_hbm, dg_hbm, qw_hbm,
    hidden_hbm, kgrad_hbm, vgrad_hbm, qwg_hbm, owg_hbm,
    probs, sgrad, q, g_all, qg, o, dg, qw, hidden, kgrad, vgrad, qwg, owg, in_sem, out_sem,
):
    pb = lax.axis_index("pb")
    slot = (pb % 2) * 4 + pb // 2
    loads = {}

    def load(name, src, dst):
        loads[name] = pltpu.make_async_copy(src, dst, in_sem.at[len(loads)])
        loads[name].start()

    load("g", g_hbm, g_all)
    for g in range(0, GROUPS, 2):
        load(("p", g), probs_hbm.at[pl.ds(g, 2)], probs.at[pl.ds(g, 2)])
    load("q", q_hbm, q)
    for g in range(0, GROUPS, 2):
        load(("s", g), sgrad_hbm.at[pl.ds(g, 2)], sgrad.at[pl.ds(g, 2)])
    load("dg", dg_hbm, dg)
    load("o", o_hbm, o)
    load("qg", qg_hbm, qg)
    load("qw", qw_hbm, qw)

    stores = []

    def store(src, dst):
        stores.append(pltpu.make_async_copy(src, dst, out_sem.at[len(stores)]))
        stores[-1].start()

    def attention_grad(low, rows, out, out_hbm, key):
        for g in range(GROUPS):
            if g % 2 == 0:
                loads[key, g].wait()
            wide = pl.ds(g * 256, 256)
            out[:, wide] = dot(low[g], head_blocks(columns(rows[pl.ds(g * 4, 4)])), NN).astype(BF16)
            if g % 2 == 1:
                both = pl.ds((g - 1) * 256, 512)
                store(out.at[:, both], out_hbm.at[:, both])

    loads["g"].wait()
    attention_grad(probs, g_all, vgrad, vgrad_hbm, "p")
    loads["q"].wait()
    attention_grad(sgrad, q, kgrad, kgrad_hbm, "s")

    def all_questions(ref, g):
        return jnp.concatenate([columns(ref[s, pl.ds(g * 4, 4)]) for s in range(PB)], axis=0)

    loads["dg"].wait()
    loads["o"].wait()
    tokens = jnp.concatenate([dg[s, 1] for s in range(PB)], axis=0)
    for g in range(GROUPS):
        owg[g * 256 : (g + 1) * 256, :] = dot(all_questions(o, g), tokens, TN)
    store(owg, owg_hbm)
    loads["qg"].wait()
    tokens = jnp.concatenate([dg[s, 0] for s in range(PB)], axis=0)
    for g in range(GROUPS):
        qwg[:, g * 256 : (g + 1) * 256] = dot(tokens, all_questions(qg, g), TN)
    store(qwg, qwg_hbm)
    loads["qw"].wait()
    hidden[...] = sum(
        dot(columns(qg[slot, pl.ds(g * 4, 4)]), qw[:, g * 256 : (g + 1) * 256], NT) for g in range(GROUPS)
    ).astype(BF16)
    store(hidden, hidden_hbm)
    for copy in stores:
        copy.wait()


def local(
    dec_hidden, out_grad, query_weight, output_weight, queries, attn_out, row_max, row_sum, keys, values, lengths
):
    hbm = pl.BlockSpec(memory_space=pl.ANY)
    sds = jax.ShapeDtypeStruct
    pieces = (PSG, 16, 128)
    probs, sgrad, q_all, g_all, qg_all, o_all, dg_all = pl.pallas_call(
        comm_kernel,
        out_shape=[
            sds((GROUPS, 512, 128), BF16), sds((GROUPS, 512, 128), BF16), sds(pieces, BF16), sds(pieces, BF16),
            sds((PB,) + pieces, BF16), sds((PB,) + pieces, BF16), sds((PB, 2, 32, 128), BF16),
        ],
        in_specs=[hbm] * 10,
        out_specs=[hbm] * 7,
        scratch_shapes=[
            pltpu.VMEM((2048, 128), BF16),
            pltpu.VMEM((512, 2048), BF16),
            pltpu.VMEM((512, 2048), BF16),
            pltpu.VMEM((1, 2048), BF16),
            pltpu.VMEM((1, 2048), BF16),
            pltpu.VMEM((1, 32), F32),
            pltpu.VMEM((1, 32), F32),
            pltpu.SMEM((1, 2), jnp.int32),
            pltpu.VMEM((32, 128), F32),
            pltpu.VMEM((PSG, 32, 128), BF16),
            pltpu.VMEM((PSG, 32, 128), F32),
            pltpu.VMEM((1, 128), F32),
            pltpu.VMEM((PSG, 1, 128), F32),
            pltpu.VMEM(pieces, BF16),
            pltpu.VMEM(pieces, BF16),
            pltpu.VMEM((16, 128), BF16),
            pltpu.VMEM(pieces, BF16),
            pltpu.VMEM(pieces, BF16),
            pltpu.VMEM((GROUPS, 512, 128), F32),
            pltpu.VMEM((GROUPS, 512, 128), BF16),
            pltpu.VMEM((GROUPS, 512, 128), BF16),
            pltpu.VMEM(pieces, BF16),
            pltpu.VMEM(pieces, BF16),
            pltpu.VMEM((16, 128), BF16),
            pltpu.VMEM((PB,) + pieces, BF16),
            pltpu.VMEM((PB,) + pieces, BF16),
            pltpu.VMEM((2, 32, 128), BF16),
            pltpu.VMEM((PB, 2, 32, 128), BF16),
            pltpu.SemaphoreType.DMA((10,)),
            pltpu.SemaphoreType.DMA((9,)),
            pltpu.SemaphoreType.DMA((9,)),
            pltpu.SemaphoreType.DMA((8,)),
            pltpu.SemaphoreType.DMA((8,)),
            pltpu.SemaphoreType.DMA((5,)),
            pltpu.SemaphoreType.DMA((5,)),
            pltpu.SemaphoreType.DMA((6,)),
            pltpu.SemaphoreType.DMA((6,)),
            pltpu.SemaphoreType.DMA((6,)),
            pltpu.SemaphoreType.DMA((10,)),
        ],
        compiler_params=pltpu.CompilerParams(collective_id=1, has_side_effects=True, vmem_limit_bytes=62 * 2**20),
        cost_estimate=pl.CostEstimate(flops=10**9, bytes_accessed=10**7, transcendentals=512 * 1024),
        name="comm",
    )(
        dec_hidden.reshape(32, 128), out_grad.reshape(32, 128), output_weight,
        queries.reshape(1, 2048), attn_out.reshape(1, 2048), row_max.reshape(1, 32), row_sum.reshape(1, 32),
        keys.reshape(512, 2048), values.reshape(512, 2048), lengths,
    )

    hidden, kgrad, vgrad, qwg, owg = pl.pallas_call(
        grads_kernel,
        out_shape=[
            sds((32, 128), BF16), sds((512, 2048), BF16), sds((512, 2048), BF16),
            sds((128, 2048), F32), sds((2048, 128), F32),
        ],
        in_specs=[hbm] * 8,
        out_specs=[hbm] * 5,
        scratch_shapes=[
            pltpu.VMEM((GROUPS, 512, 128), BF16),
            pltpu.VMEM((GROUPS, 512, 128), BF16),
            pltpu.VMEM(pieces, BF16),
            pltpu.VMEM(pieces, BF16),
            pltpu.VMEM((PB,) + pieces, BF16),
            pltpu.VMEM((PB,) + pieces, BF16),
            pltpu.VMEM((PB, 2, 32, 128), BF16),
            pltpu.VMEM((128, 2048), BF16),
            pltpu.VMEM((32, 128), BF16),
            pltpu.VMEM((512, 2048), BF16),
            pltpu.VMEM((512, 2048), BF16),
            pltpu.VMEM((128, 2048), F32),
            pltpu.VMEM((2048, 128), F32),
            pltpu.SemaphoreType.DMA((14,)),
            pltpu.SemaphoreType.DMA((11,)),
        ],
        compiler_params=pltpu.CompilerParams(vmem_limit_bytes=62 * 2**20),
        cost_estimate=pl.CostEstimate(flops=10**9, bytes_accessed=10**7, transcendentals=0),
        name="grads",
    )(probs, sgrad, q_all, g_all, qg_all, o_all, dg_all, query_weight)
    return (
        hidden.reshape(dec_hidden.shape), kgrad.reshape(keys.shape), vgrad.reshape(values.shape), qwg, owg
    )


def solution(mesh):
    in_specs = (
        P("pb", None, "psg"),
        P("pb", None, "psg"),
        P("psg", None),
        P(None, "psg"),
        P("pb", "psg", None),
        P("pb", "psg", None),
        P("pb", "psg", None),
        P("pb", "psg", None),
        P("pb", "psg", None, None),
        P("pb", "psg", None, None),
        P("pb", "psg"),
    )
    out_specs = (
        P("pb", None, "psg"),
        P("pb", "psg", None, None),
        P("pb", "psg", None, None),
        P("psg", None),
        P(None, "psg"),
    )
    return jax.shard_map(local, mesh=mesh, in_specs=in_specs, out_specs=out_specs, check_vma=False)
```

time: 62.2 us -> 53.2 us (0.86)
  Pallas kernels: 61.3 us -> 52.4 us
    pallas_call x2, Pallas kernels: 61.3 us -> 52.4 us  [the longest x1 47 us: local(): pl.pallas_call(comm_kernel, out_shape=[sds((GROUPS, 512, 128), BF16), sds...]
where the time goes in v2:
time: 53.2 us; the launch traced here: 53 us
  Pallas kernels  52.4 us (98%)
  between operations  0.64 us (1%)
    pallas_call x1, Pallas kernels, local(): pl.pallas_call(comm_kernel, out_shape=[sds((GROUPS, 512, 128), BF16), sds...  47 us
    pallas_call x1, Pallas kernels, local(): pl.pallas_call(grads_kernel, out_shape=[sds((32, 128), BF16), sds((512, 2...  5.43 us

profile of v2, /device:TPU:1, one launch (start us, length us, event | category | flops | bytes accessed | tf_op | source)
XLA Modules:
  0.0 53.0 jit_solution(1761672074992106461)
XLA Ops:
  0.6 47.0 %comm.1 = (bf16[8,512,128]{2,1,0:T(8,128)(2,1)}, bf16[8,512,128]{2,1,0:T(8,128)(2,1)}, bf16[32,16,128]{2,1,0:T(8,128)(2,1)}, bf16[32,16,128]{2,1,0:T(8,128)(2,1)...) custom-call(bf16[32,128]{1,0:T(8,128)(2,1)} %bitcast.13, ...), custom_call_target="tpu_custom_call" | custom-call | flops 1000000000 | bytes 10000000 | tf_op jit(solution)/shard_map/comm/pallas_call | solution.py:355
  47.6 5.4 %grads.1 = (bf16[32,128]{1,0:T(8,128)(2,1)}, bf16[512,2048]{1,0:T(8,128)(2,1)}, bf16[512,2048]{1,0:T(8,128)(2,1)}, f32[128,2048]{1,0:T(8,128)}, f32[2048,128]{1,0:T(8,128)}) custom-call(bf16[8,512,128]{2,1,0:T(8,128)(2,1)} %get-tuple-element.17.probs_hbm, bf16[8,512,128]{2,1,0:T(8,128)(2,1)} %get-tuple-element.18.sgrad_hbm, ...), custom_call_target="tpu_custom_call" | custom-call | flops 1000000000 | bytes 10000000 | tf_op jit(solution)/shard_map/grads/pallas_call | solution.py:413

commit v3 on v2

--- a/solution.py
+++ b/solution.py
@@ -46,15 +46,16 @@
 
 def comm_kernel(
     dec_hbm, grad_hbm, weight_hbm, query_hbm, attn_hbm, max_hbm, sum_hbm, keys_hbm, values_hbm, len_hbm,
-    probs_out, sgrad_out, q_out, g_out, qg_out, o_out, dg_out,
+    kgrad_out, vgrad_out, owg_out, qg_out, dg_out, q_out,
     weight, keys, values, query_ref, attn_ref, max_ref, sum_ref, len_ref, bundle, qa, qa32, stat_src, stats,
-    partial, part_in, g_own, g_all, q_all, probs, probs_low, sgrad, qpart, qpart_in, qg_own, qg_all,
+    partial, part_in, g_own, g_all, q_all, probs, probs_low, sgrad, vgrad, owg, qpart, qpart_in, qg_own, qg_all,
     o_all, dg_src, dg_all,
     local_sem, send_sem, recv_sem, x_send, x_recv, side_send, side_recv, core_send,
-    core_recv, out_sem, qg_sem,
+    core_recv, out_sem,
 ):
     me, pb = lax.axis_index("psg"), lax.axis_index("pb")
     z, y = lax.div(me, Y), lax.rem(me, Y)
+    half_of = lax.div(z, 4)
     core, xpos = lax.rem(pb, 2), lax.div(pb, 2)
     slot = core * 4 + xpos
     partner = pb + 1 - 2 * core
@@ -111,11 +112,11 @@
     def wait_bytes(ref, sem):
         pltpu.make_async_copy(ref, ref, sem).wait()
 
+    for to in far_first:
+        send(partial.at[to], part_in.at[me], send_sem.at[0], recv_sem.at[0], (to, pb))
+    part_in[me] = partial[me]
     for dy in (2, 1, 3):
         send(stats.at[me], stats.at[me], send_sem.at[2], recv_sem.at[2], (peers[0, dy], pb))
-    for to in far_first:
-        send(partial.at[to], part_in.at[me], send_sem.at[0], recv_sem.at[0], (to, pb))
-    part_in[me] = partial[me]
     for to in far_first:
         send(qa.at[me], qa.at[me], send_sem.at[1], recv_sem.at[1], (to, pb))
     row_of_four = pl.ds(z * Y, Y)
@@ -129,7 +130,7 @@
         send(g_own, g_all.at[me], send_sem.at[3], recv_sem.at[3], (to, pb))
     g_all[me] = g_own[...]
     for d in range(1, PB):
-        send(dg_src, dg_all.at[slot], x_send.at[7], x_recv.at[7], (me, pb_peers[d]))
+        send(dg_src, dg_all.at[slot], x_send.at[1], x_recv.at[4], (me, pb_peers[d]))
 
     wait_bytes(qa.at[pl.ds(0, PSG - 1)], recv_sem.at[1])
     qa32[...] = qa[...].astype(F32)
@@ -142,10 +143,8 @@
         o_all[slot, 2 * k + 1] = block[16:32]
     own = o_all.at[slot]
     for d in range(1, 4):
-        send(own, own, x_send.at[d], x_recv.at[d], (me, pb_peers[2 * d]))
+        send(own, own, x_send.at[0], x_recv.at[d], (me, pb_peers[2 * d]))
     send(own, own, x_send.at[0], x_recv.at[0], (me, partner))
-    q_copy = pltpu.make_async_copy(q_all, q_out, out_sem.at[0])
-    q_copy.start()
 
     wait_bytes(stats.at[pl.ds(0, PSG - Y)], recv_sem.at[5])
     stat_rows = jnp.concatenate([stats[t] for t in range(PSG)], axis=0)
@@ -167,8 +166,6 @@
             value = jnp.where(position < len_ref[0, p], jnp.exp(scores[p * 256 : (p + 1) * 256]), 0.0)
             probs[g, rows] = value
             probs_low[g, rows] = value.astype(BF16)
-    probs_copy = pltpu.make_async_copy(probs_low, probs_out, out_sem.at[1])
-    probs_copy.start()
     values_copy.wait()
 
     wait_bytes(g_all.at[pl.ds(0, PSG - 1)], recv_sem.at[3])
@@ -193,17 +190,23 @@
     for to in far_first:
         send(qpart.at[to], qpart_in.at[me], send_sem.at[4], recv_sem.at[4], (to, pb))
     qpart_in[me] = qpart[me]
-    g_copy = pltpu.make_async_copy(g_all, g_out, out_sem.at[2])
-    g_copy.start()
-    sgrad_copy = pltpu.make_async_copy(sgrad, sgrad_out, out_sem.at[3])
-    sgrad_copy.start()
+
+    for g in range(GROUPS):
+        wide, four = pl.ds(g * 256, 256), pl.ds(g * 4, 4)
+        vgrad[:, wide] = dot(probs_low[g], head_blocks(columns(g_all[four])), NN).astype(BF16)
+    vgrad_copy = pltpu.make_async_copy(vgrad, vgrad_out, out_sem.at[0])
+    vgrad_copy.start()
+    kgrad_copy = pltpu.make_async_copy(sgrad, kgrad_out, out_sem.at[1])
+    kgrad_copy.start()
+    q_copy = pltpu.make_async_copy(q_all, q_out, out_sem.at[5])
+    q_copy.start()
 
     for d in (1, 3, 2):
         wait_bytes(own, x_recv.at[d])
         got = o_all.at[core * 4 + lax.rem(xpos + 4 - d, 4)]
-        send(got, got, x_send.at[3 + d], x_recv.at[3 + d], (me, partner))
-    wait_bytes(dg_all.at[pl.ds(0, PB - 1)], x_recv.at[7])
-    dg_copy = pltpu.make_async_copy(dg_all, dg_out, out_sem.at[4])
+        send(got, got, x_send.at[0], x_recv.at[0], (me, partner))
+    wait_bytes(dg_all.at[pl.ds(0, PB - 1)], x_recv.at[4])
+    dg_copy = pltpu.make_async_copy(dg_all, dg_out, out_sem.at[2])
     dg_copy.start()
 
     wait_bytes(qpart_in.at[pl.ds(0, PSG - 1)], recv_sem.at[4])
@@ -211,139 +214,117 @@
     opposite = core * 4 + lax.rem(xpos + 2, 4)
     send(qg_own, qg_all.at[slot, me], side_send.at[0], side_recv.at[0], (me, pb_peers[4]))
     for to in far_first:
-        send(qg_own, qg_all.at[slot, me], send_sem.at[5], recv_sem.at[7], (to, pb))
+        send(qg_own, qg_all.at[slot, me], send_sem.at[5], recv_sem.at[6 + half_of], (to, pb))
     qg_all[slot, me] = qg_own[...]
     wait_bytes(qg_own, side_recv.at[0])
     for to in far_first:
         send(qg_all.at[opposite, me], qg_all.at[opposite, me], send_sem.at[6], recv_sem.at[8], (to, pb))
 
-    for k in (0, 4, 6, 5):
-        wait_bytes(own, x_recv.at[k])
-    o_copy = pltpu.make_async_copy(o_all, o_out, out_sem.at[5])
-    o_copy.start()
-    copies = []
-
+    wait_bytes(o_all.at[pl.ds(0, 4)], x_recv.at[0])
+    tokens = jnp.concatenate([dg_all[s, 1] for s in range(PB)], axis=0)
+    for g in range(GROUPS):
+        rows = jnp.concatenate([columns(o_all[s, pl.ds(g * 4, 4)]) for s in range(PB)], axis=0)
+        owg[g * 256 : (g + 1) * 256, :] = dot(rows, tokens, TN)
+    owg_copy = pltpu.make_async_copy(owg, owg_out, out_sem.at[3])
+    owg_copy.start()
     for i, count, ref in (
         (0, PSG - 1, partial), (1, PSG - 1, qa), (2, Y - 1, stats), (3, PSG - 1, g_all), (4, PSG - 1, qpart),
         (5, PSG - 1, qpart), (7, PSG - Y, stats),
     ):
         wait_bytes(ref.at[pl.ds(0, count)], send_sem.at[i])
-    for k in range(7):
-        wait_bytes(own, x_send.at[k])
-    wait_bytes(dg_all.at[pl.ds(0, PB - 1)], x_send.at[7])
+    wait_bytes(o_all.at[pl.ds(0, 7)], x_send.at[0])
+    wait_bytes(dg_all.at[pl.ds(0, PB - 1)], x_send.at[1])
     wait_bytes(qg_own, side_send.at[0])
-    for copy in (q_copy, probs_copy, g_copy, sgrad_copy, dg_copy, o_copy):
+    for copy in (vgrad_copy, kgrad_copy, dg_copy, owg_copy, q_copy):
         copy.wait()
 
-    def keep(at, first, count):
+    def keep(at):
+        pltpu.make_async_copy(qg_all.at[at], qg_out.at[at], out_sem.at[5]).start()
+
+    def hand_over(at, first, count):
         part = pl.ds(first, count)
-        copies.append(pltpu.make_async_copy(qg_all.at[at, part], qg_out.at[at, part], qg_sem.at[len(copies)]))
-        copies[-1].start()
-
-    def hand_over(at, first, count, k):
-        part = qg_all.at[at, pl.ds(first, count)]
-        send(part, part, core_send.at[k], core_recv.at[k], (me, partner))
-
-    wait_bytes(qg_all.at[slot, pl.ds(0, PSG - 1)], recv_sem.at[7])
-    for half in range(2):
-        part = qg_all.at[slot, pl.ds(16 * half, 16)]
-        for i, d in enumerate((2, 6)):
-            send(part, part, side_send.at[1 + 2 * half + i], side_recv.at[1 + 2 * half + i], (me, pb_peers[d]))
-    hand_over(slot, 0, PSG, 0)
-    keep(slot, 0, PSG)
+        send(qg_all.at[at, part], qg_out.at[at, part], core_send.at[0], core_recv.at[0], (me, partner))
+
+    firsts = (16 * half_of, 16 - 16 * half_of)
+    for half, first in enumerate(firsts):
+        wait_bytes(qg_all.at[slot, pl.ds(0, 15 + half)], recv_sem.at[6 + half_of if half == 0 else 7 - half_of])
+        part = qg_all.at[slot, pl.ds(first, 16)]
+        for d in (2, 6):
+            send(part, part, side_send.at[1], side_recv.at[1 + half], (me, pb_peers[d]))
+    hand_over(slot, 0, PSG)
+    keep(slot)
     wait_bytes(qg_all.at[slot, pl.ds(0, PSG - 1)], recv_sem.at[8])
-    hand_over(opposite, 0, PSG, 1)
-    keep(opposite, 0, PSG)
+    hand_over(opposite, 0, PSG)
+    keep(opposite)
     sides = [core * 4 + lax.rem(xpos + d, 4) for d in (3, 1)]
     for half in range(2):
-        for i in range(2):
-            wait_bytes(qg_all.at[slot, pl.ds(0, 16)], side_recv.at[1 + 2 * half + i])
-            hand_over(sides[i], 16 * half, 16, 2 + 2 * half + i)
-    for i in range(2):
-        keep(sides[i], 0, PSG)
-    for k, d in enumerate((0, 2)):
-        wait_bytes(qg_all.at[slot], core_recv.at[k])
-        keep(lax.rem(slot + 4, PB) if d == 0 else lax.rem(opposite + 4, PB), 0, PSG)
-    for half in range(2):
-        for i in range(2):
-            wait_bytes(qg_all.at[slot, pl.ds(0, 16)], core_recv.at[2 + 2 * half + i])
-            keep(lax.rem(sides[i] + 4, PB), 16 * half, 16)
-
+        wait_bytes(qg_all.at[slot], side_recv.at[1 + half])
+        for at in sides:
+            hand_over(at, firsts[half], 16)
+    for at in sides:
+        keep(at)
     wait_bytes(qpart.at[pl.ds(0, PSG - 1)], send_sem.at[6])
-    for k in range(1, 5):
-        wait_bytes(qg_all.at[slot, pl.ds(0, 16)], side_send.at[k])
-    for k in range(6):
-        wait_bytes(qg_all.at[slot, pl.ds(0, PSG if k < 2 else 16)], core_send.at[k])
-    for copy in copies:
-        copy.wait()
+    wait_bytes(qg_all.at[pl.ds(0, 2)], side_send.at[1])
+    wait_bytes(qg_all.at[pl.ds(0, 4)], core_send.at[0])
+    wait_bytes(qg_all.at[pl.ds(0, 4)], out_sem.at[5])
+    wait_bytes(qg_all.at[pl.ds(0, 4)], core_recv.at[0])
 
 
 def grads_kernel(
-    probs_hbm, sgrad_hbm, q_hbm, g_hbm, qg_hbm, o_hbm, dg_hbm, qw_hbm,
-    hidden_hbm, kgrad_hbm, vgrad_hbm, qwg_hbm, owg_hbm,
-    probs, sgrad, q, g_all, qg, o, dg, qw, hidden, kgrad, vgrad, qwg, owg, in_sem, out_sem,
+    kgrad_in, vgrad_in, owg_in, qg_hbm, dg_hbm, qw_hbm, q_hbm, hidden_hbm, kgrad_out, vgrad_out, qwg_hbm, owg_out,
+    sgrad, kgrad, vgrad, owg, qg, dg, qw, q_all, hidden, qwg, in_sem, out_sem,
 ):
     pb = lax.axis_index("pb")
     slot = (pb % 2) * 4 + pb // 2
-    loads = {}
-
-    def load(name, src, dst):
-        loads[name] = pltpu.make_async_copy(src, dst, in_sem.at[len(loads)])
-        loads[name].start()
-
-    load("g", g_hbm, g_all)
-    for g in range(0, GROUPS, 2):
-        load(("p", g), probs_hbm.at[pl.ds(g, 2)], probs.at[pl.ds(g, 2)])
-    load("q", q_hbm, q)
-    for g in range(0, GROUPS, 2):
-        load(("s", g), sgrad_hbm.at[pl.ds(g, 2)], sgrad.at[pl.ds(g, 2)])
-    load("dg", dg_hbm, dg)
-    load("o", o_hbm, o)
-    load("qg", qg_hbm, qg)
-    load("qw", qw_hbm, qw)
-
-    stores = []
-
-    def store(src, dst):
-        stores.append(pltpu.make_async_copy(src, dst, out_sem.at[len(stores)]))
-        stores[-1].start()
-
-    def attention_grad(low, rows, out, out_hbm, key):
-        for g in range(GROUPS):
-            if g % 2 == 0:
-                loads[key, g].wait()
-            wide = pl.ds(g * 256, 256)
-            out[:, wide] = dot(low[g], head_blocks(columns(rows[pl.ds(g * 4, 4)])), NN).astype(BF16)
-            if g % 2 == 1:
-                both = pl.ds((g - 1) * 256, 512)
-                store(out.at[:, both], out_hbm.at[:, both])
-
-    loads["g"].wait()
-    attention_grad(probs, g_all, vgrad, vgrad_hbm, "p")
-    loads["q"].wait()
-    attention_grad(sgrad, q, kgrad, kgrad_hbm, "s")
-
-    def all_questions(ref, g):
-        return jnp.concatenate([columns(ref[s, pl.ds(g * 4, 4)]) for s in range(PB)], axis=0)
-
-    loads["dg"].wait()
-    loads["o"].wait()
-    tokens = jnp.concatenate([dg[s, 1] for s in range(PB)], axis=0)
-    for g in range(GROUPS):
-        owg[g * 256 : (g + 1) * 256, :] = dot(all_questions(o, g), tokens, TN)
-    store(owg, owg_hbm)
-    loads["qg"].wait()
+    loads = []
+
+    def load(src, dst):
+        loads.append(pltpu.make_async_copy(src, dst, in_sem.at[len(loads)]))
+        loads[-1].start()
+        return loads[-1]
+
+    def store(i, src, dst):
+        pltpu.make_async_copy(src, dst, out_sem.at[i]).start()
+
+    q_load = load(q_hbm, q_all)
+    k_loads = [load(kgrad_in.at[pl.ds(g, 2)], sgrad.at[pl.ds(g, 2)]) for g in range(0, GROUPS, 2)]
+    v_loads = [load(vgrad_in.at[pl.ds(i * 256, 256)], vgrad.at[pl.ds(i * 256, 256)]) for i in range(2)]
+    dg_load = load(dg_hbm, dg)
+    qg_load = load(qg_hbm, qg)
+    qw_load = load(qw_hbm, qw)
+    owg_load = load(owg_in, owg)
+
+    q_load.wait()
+    for g in range(GROUPS):
+        if g % 2 == 0:
+            k_loads[g // 2].wait()
+        wide, four = pl.ds(g * 256, 256), pl.ds(g * 4, 4)
+        kgrad[:, wide] = dot(sgrad[g], head_blocks(columns(q_all[four])), NN).astype(BF16)
+        if g % 2 == 1:
+            both = pl.ds((g - 1) * 256, 512)
+            store(1, kgrad.at[:, both], kgrad_out.at[:, both])
+    for i in range(2):
+        rows = pl.ds(i * 256, 256)
+        v_loads[i].wait()
+        store(0, vgrad.at[rows], vgrad_out.at[rows])
+    dg_load.wait()
+    qg_load.wait()
     tokens = jnp.concatenate([dg[s, 0] for s in range(PB)], axis=0)
     for g in range(GROUPS):
-        qwg[:, g * 256 : (g + 1) * 256] = dot(tokens, all_questions(qg, g), TN)
-    store(qwg, qwg_hbm)
-    loads["qw"].wait()
+        wide, four = pl.ds(g * 256, 256), pl.ds(g * 4, 4)
+        qwg[:, wide] = dot(tokens, jnp.concatenate([columns(qg[s, four]) for s in range(PB)], axis=0), TN)
+        if g % 4 == 3:
+            half = pl.ds((g - 3) * 256, 1024)
+            store(2, qwg.at[:, half], qwg_hbm.at[:, half])
+    owg_load.wait()
+    store(3, owg, owg_out)
+    qw_load.wait()
     hidden[...] = sum(
         dot(columns(qg[slot, pl.ds(g * 4, 4)]), qw[:, g * 256 : (g + 1) * 256], NT) for g in range(GROUPS)
     ).astype(BF16)
-    store(hidden, hidden_hbm)
-    for copy in stores:
-        copy.wait()
+    store(4, hidden, hidden_hbm)
+    for i, ref in enumerate((vgrad, kgrad, qwg, owg, hidden)):
+        pltpu.make_async_copy(ref, ref, out_sem.at[i]).wait()
 
 
 def local(
@@ -352,14 +333,14 @@
     hbm = pl.BlockSpec(memory_space=pl.ANY)
     sds = jax.ShapeDtypeStruct
     pieces = (PSG, 16, 128)
-    probs, sgrad, q_all, g_all, qg_all, o_all, dg_all = pl.pallas_call(
+    kgrad, vgrad, owg, qg_all, dg_all, q_all = pl.pallas_call(
         comm_kernel,
         out_shape=[
-            sds((GROUPS, 512, 128), BF16), sds((GROUPS, 512, 128), BF16), sds(pieces, BF16), sds(pieces, BF16),
-            sds((PB,) + pieces, BF16), sds((PB,) + pieces, BF16), sds((PB, 2, 32, 128), BF16),
+            sds((GROUPS, 512, 128), BF16), sds((512, 2048), BF16), sds((2048, 128), F32),
+            sds((PB,) + pieces, BF16), sds((PB, 2, 32, 128), BF16), sds(pieces, BF16),
         ],
         in_specs=[hbm] * 10,
-        out_specs=[hbm] * 7,
+        out_specs=[hbm] * 6,
         scratch_shapes=[
             pltpu.VMEM((2048, 128), BF16),
             pltpu.VMEM((512, 2048), BF16),
@@ -382,6 +363,8 @@
             pltpu.VMEM((GROUPS, 512, 128), F32),
             pltpu.VMEM((GROUPS, 512, 128), BF16),
             pltpu.VMEM((GROUPS, 512, 128), BF16),
+            pltpu.VMEM((512, 2048), BF16),
+            pltpu.VMEM((2048, 128), F32),
             pltpu.VMEM(pieces, BF16),
             pltpu.VMEM(pieces, BF16),
             pltpu.VMEM((16, 128), BF16),
@@ -390,16 +373,15 @@
             pltpu.VMEM((2, 32, 128), BF16),
             pltpu.VMEM((PB, 2, 32, 128), BF16),
             pltpu.SemaphoreType.DMA((10,)),
+            pltpu.SemaphoreType.DMA((8,)),
             pltpu.SemaphoreType.DMA((9,)),
-            pltpu.SemaphoreType.DMA((9,)),
-            pltpu.SemaphoreType.DMA((8,)),
-            pltpu.SemaphoreType.DMA((8,)),
+            pltpu.SemaphoreType.DMA((2,)),
             pltpu.SemaphoreType.DMA((5,)),
-            pltpu.SemaphoreType.DMA((5,)),
+            pltpu.SemaphoreType.DMA((2,)),
+            pltpu.SemaphoreType.DMA((3,)),
+            pltpu.SemaphoreType.DMA((1,)),
+            pltpu.SemaphoreType.DMA((1,)),
             pltpu.SemaphoreType.DMA((6,)),
-            pltpu.SemaphoreType.DMA((6,)),
-            pltpu.SemaphoreType.DMA((6,)),
-            pltpu.SemaphoreType.DMA((10,)),
         ],
         compiler_params=pltpu.CompilerParams(collective_id=1, has_side_effects=True, vmem_limit_bytes=62 * 2**20),
         cost_estimate=pl.CostEstimate(flops=10**9, bytes_accessed=10**7, transcendentals=512 * 1024),
@@ -416,29 +398,26 @@
             sds((32, 128), BF16), sds((512, 2048), BF16), sds((512, 2048), BF16),
             sds((128, 2048), F32), sds((2048, 128), F32),
         ],
-        in_specs=[hbm] * 8,
+        in_specs=[hbm] * 7,
         out_specs=[hbm] * 5,
         scratch_shapes=[
             pltpu.VMEM((GROUPS, 512, 128), BF16),
-            pltpu.VMEM((GROUPS, 512, 128), BF16),
-            pltpu.VMEM(pieces, BF16),
-            pltpu.VMEM(pieces, BF16),
-            pltpu.VMEM((PB,) + pieces, BF16),
+            pltpu.VMEM((512, 2048), BF16),
+            pltpu.VMEM((512, 2048), BF16),
+            pltpu.VMEM((2048, 128), F32),
             pltpu.VMEM((PB,) + pieces, BF16),
             pltpu.VMEM((PB, 2, 32, 128), BF16),
             pltpu.VMEM((128, 2048), BF16),
+            pltpu.VMEM(pieces, BF16),
             pltpu.VMEM((32, 128), BF16),
-            pltpu.VMEM((512, 2048), BF16),
-            pltpu.VMEM((512, 2048), BF16),
             pltpu.VMEM((128, 2048), F32),
-            pltpu.VMEM((2048, 128), F32),
             pltpu.SemaphoreType.DMA((14,)),
-            pltpu.SemaphoreType.DMA((11,)),
+            pltpu.SemaphoreType.DMA((5,)),
         ],
         compiler_params=pltpu.CompilerParams(vmem_limit_bytes=62 * 2**20),
         cost_estimate=pl.CostEstimate(flops=10**9, bytes_accessed=10**7, transcendentals=0),
         name="grads",
-    )(probs, sgrad, q_all, g_all, qg_all, o_all, dg_all, query_weight)
+    )(kgrad, vgrad, owg, qg_all, dg_all, query_weight, q_all)
     return (
         hidden.reshape(dec_hidden.shape), kgrad.reshape(keys.shape), vgrad.reshape(values.shape), qwg, owg
     )

time: 53.2 us -> 51.5 us (0.968)
  Pallas kernels: 52.4 us -> 50.7 us
    pallas_call x1, Pallas kernels: 47 us -> 46 us  [local(): pl.pallas_call(comm_kernel, out_shape=[sds((GROUPS, 512, 128), BF16), sds...]
    pallas_call x1, Pallas kernels: 5.43 us -> 4.77 us  [local(): pl.pallas_call(grads_kernel, out_shape=[sds((32, 128), BF16), sds((512, 2...]
where the time goes in v3:
time: 51.5 us; the launch traced here: 51.4 us
  Pallas kernels  50.7 us (98%)
  between operations  0.64 us (1%)
    pallas_call x1, Pallas kernels, local(): pl.pallas_call(comm_kernel, out_shape=[sds((GROUPS, 512, 128), BF16), sds...  46 us
    pallas_call x1, Pallas kernels, local(): pl.pallas_call(grads_kernel, out_shape=[sds((32, 128), BF16), sds((512, 2...  4.77 us

profile of v3, /device:TPU:1, one launch (start us, length us, event | category | flops | bytes accessed | tf_op | source)
XLA Modules:
  0.0 51.4 jit_solution(15766497722983326209)
XLA Ops:
  0.6 46.0 %comm.1 = (bf16[8,512,128]{2,1,0:T(8,128)(2,1)}, bf16[512,2048]{1,0:T(8,128)(2,1)}, f32[2048,128]{1,0:T(8,128)}, bf16[8,32,16,128]{3,2,1,0:T(8,128)(2,1)}, bf16[...) custom-call(bf16[32,128]{1,0:T(8,128)(2,1)} %bitcast.13, bf16[32,128]{1,0:T(8,128)(2,1)} %bitcast.14, ...), custom_call_target="tpu_custom_call" | custom-call | flops 1000000000 | bytes 10000000 | tf_op jit(solution)/shard_map/comm/pallas_call | solution.py:336
  46.6 4.8 %grads.1 = (bf16[32,128]{1,0:T(8,128)(2,1)}, bf16[512,2048]{1,0:T(8,128)(2,1)}, bf16[512,2048]{1,0:T(8,128)(2,1)}, f32[128,2048]{1,0:T(8,128)}, f32[2048,128]{1,0:T(8,128)}) custom-call(bf16[8,512,128]{2,1,0:T(8,128)(2,1)} %get-tuple-element.16.kgrad_in, bf16[512,2048]{1,0:T(8,128)(2,1)} %get-tuple-element.17.vgrad_in, ...), custom_call_target="tpu_custom_call" | custom-call | flops 1000000000 | bytes 10000000 | tf_op jit(solution)/shard_map/grads/pallas_call | solution.py:395

commit v4 on v3

--- a/solution.py
+++ b/solution.py
@@ -88,7 +88,8 @@
     for k in range(16):
         bundle[k : k + 1, :] = query_ref[:, k * 128 : (k + 1) * 128].astype(F32)
         bundle[16 + k : 17 + k, :] = attn_ref[:, k * 128 : (k + 1) * 128].astype(F32)
-    qa[me] = bundle[...].astype(BF16)
+    qa[0, me] = bundle[0:16].astype(BF16)
+    qa[1, me] = bundle[16:32].astype(BF16)
     stat_src[...] = jnp.zeros_like(stat_src)
     stat_src[0:1, 0:32] = max_ref[...] + jnp.log(sum_ref[...])
     stats[me] = stat_src[...]
@@ -116,9 +117,10 @@
         send(partial.at[to], part_in.at[me], send_sem.at[0], recv_sem.at[0], (to, pb))
     part_in[me] = partial[me]
     for dy in (2, 1, 3):
+        send(qa.at[1, me], qa.at[1, me], send_sem.at[8], recv_sem.at[9], (peers[0, dy], pb))
         send(stats.at[me], stats.at[me], send_sem.at[2], recv_sem.at[2], (peers[0, dy], pb))
     for to in far_first:
-        send(qa.at[me], qa.at[me], send_sem.at[1], recv_sem.at[1], (to, pb))
+        send(qa.at[0, me], qa.at[0, me], send_sem.at[1], recv_sem.at[1], (to, pb))
     row_of_four = pl.ds(z * Y, Y)
     wait_bytes(stats.at[pl.ds(0, Y - 1)], recv_sem.at[2])
     for dz in (4, 5, 3, 6, 2, 7, 1):
@@ -129,22 +131,19 @@
     for to in far_first:
         send(g_own, g_all.at[me], send_sem.at[3], recv_sem.at[3], (to, pb))
     g_all[me] = g_own[...]
+    wait_bytes(qa.at[1, pl.ds(0, Y - 1)], recv_sem.at[9])
+    for dz in (4, 5, 3, 6, 2, 7, 1):
+        rows = qa.at[1, row_of_four]
+        send(rows, rows, send_sem.at[9], recv_sem.at[10], (peers[dz, 0], pb))
     for d in range(1, PB):
         send(dg_src, dg_all.at[slot], x_send.at[1], x_recv.at[4], (me, pb_peers[d]))
 
-    wait_bytes(qa.at[pl.ds(0, PSG - 1)], recv_sem.at[1])
-    qa32[...] = qa[...].astype(F32)
+    wait_bytes(qa.at[0, pl.ds(0, PSG - 1)], recv_sem.at[1])
+    qa32[...] = qa[0].astype(F32)
     for k in range(16):
         block = qa32[:, k, :].astype(BF16)
         q_all[2 * k] = block[0:16]
         q_all[2 * k + 1] = block[16:32]
-        block = qa32[:, 16 + k, :].astype(BF16)
-        o_all[slot, 2 * k] = block[0:16]
-        o_all[slot, 2 * k + 1] = block[16:32]
-    own = o_all.at[slot]
-    for d in range(1, 4):
-        send(own, own, x_send.at[0], x_recv.at[d], (me, pb_peers[2 * d]))
-    send(own, own, x_send.at[0], x_recv.at[0], (me, partner))
 
     wait_bytes(stats.at[pl.ds(0, PSG - Y)], recv_sem.at[5])
     stat_rows = jnp.concatenate([stats[t] for t in range(PSG)], axis=0)
@@ -166,6 +165,17 @@
             value = jnp.where(position < len_ref[0, p], jnp.exp(scores[p * 256 : (p + 1) * 256]), 0.0)
             probs[g, rows] = value
             probs_low[g, rows] = value.astype(BF16)
+    wait_bytes(qa.at[1, pl.ds(0, PSG - Y)], recv_sem.at[10])
+    qa32[...] = qa[1].astype(F32)
+    for k in range(16):
+        block = qa32[:, k, :].astype(BF16)
+        o_all[slot, 2 * k] = block[0:16]
+        o_all[slot, 2 * k + 1] = block[16:32]
+    own = o_all.at[slot]
+    for d in range(1, 4):
+        send(own, own, x_send.at[0], x_recv.at[d], (me, pb_peers[2 * d]))
+    send(own, own, x_send.at[0], x_recv.at[0], (me, partner))
+
     values_copy.wait()
 
     wait_bytes(g_all.at[pl.ds(0, PSG - 1)], recv_sem.at[3])
@@ -228,7 +238,7 @@
     owg_copy = pltpu.make_async_copy(owg, owg_out, out_sem.at[3])
     owg_copy.start()
     for i, count, ref in (
-        (0, PSG - 1, partial), (1, PSG - 1, qa), (2, Y - 1, stats), (3, PSG - 1, g_all), (4, PSG - 1, qpart),
+        (0, PSG - 1, partial), (1, PSG - 1, qa.at[0]), (2, Y - 1, stats), (8, Y - 1, qa.at[1]), (9, PSG - Y, qa.at[1]), (3, PSG - 1, g_all), (4, PSG - 1, qpart),
         (5, PSG - 1, qpart), (7, PSG - Y, stats),
     ):
         wait_bytes(ref.at[pl.ds(0, count)], send_sem.at[i])
@@ -238,8 +248,9 @@
     for copy in (vgrad_copy, kgrad_copy, dg_copy, owg_copy, q_copy):
         copy.wait()
 
-    def keep(at):
-        pltpu.make_async_copy(qg_all.at[at], qg_out.at[at], out_sem.at[5]).start()
+    def keep(at, first=0, count=PSG):
+        part = pl.ds(first, count)
+        pltpu.make_async_copy(qg_all.at[at, part], qg_out.at[at, part], out_sem.at[5]).start()
 
     def hand_over(at, first, count):
         part = pl.ds(first, count)
@@ -248,26 +259,32 @@
     firsts = (16 * half_of, 16 - 16 * half_of)
     for half, first in enumerate(firsts):
         wait_bytes(qg_all.at[slot, pl.ds(0, 15 + half)], recv_sem.at[6 + half_of if half == 0 else 7 - half_of])
-        part = qg_all.at[slot, pl.ds(first, 16)]
-        for d in (2, 6):
-            send(part, part, side_send.at[1], side_recv.at[1 + half], (me, pb_peers[d]))
+        span = pl.ds(first, 16)
+        part = qg_all.at[slot, span]
+        if half == 0:
+            for d in (2, 6):
+                send(part, part, side_send.at[1], side_recv.at[1], (me, pb_peers[d]))
+        else:
+            for d in (2, 6):
+                for to in (pb_peers[d], lax.rem(partner + d, PB)):
+                    send(part, qg_out.at[slot, span], side_send.at[1], side_recv.at[2], (me, to))
     hand_over(slot, 0, PSG)
     keep(slot)
     wait_bytes(qg_all.at[slot, pl.ds(0, PSG - 1)], recv_sem.at[8])
     hand_over(opposite, 0, PSG)
     keep(opposite)
     sides = [core * 4 + lax.rem(xpos + d, 4) for d in (3, 1)]
-    for half in range(2):
-        wait_bytes(qg_all.at[slot], side_recv.at[1 + half])
-        for at in sides:
-            hand_over(at, firsts[half], 16)
+    wait_bytes(qg_all.at[slot], side_recv.at[1])
     for at in sides:
-        keep(at)
+        hand_over(at, firsts[0], 16)
+    for at in sides:
+        keep(at, firsts[0], 16)
     wait_bytes(qpart.at[pl.ds(0, PSG - 1)], send_sem.at[6])
-    wait_bytes(qg_all.at[pl.ds(0, 2)], side_send.at[1])
-    wait_bytes(qg_all.at[pl.ds(0, 4)], core_send.at[0])
-    wait_bytes(qg_all.at[pl.ds(0, 4)], out_sem.at[5])
-    wait_bytes(qg_all.at[pl.ds(0, 4)], core_recv.at[0])
+    wait_bytes(qg_all.at[pl.ds(0, 3)], side_send.at[1])
+    wait_bytes(qg_all.at[pl.ds(0, 3)], core_send.at[0])
+    wait_bytes(qg_all.at[pl.ds(0, 3)], out_sem.at[5])
+    wait_bytes(qg_all.at[pl.ds(0, 2)], side_recv.at[2])
+    wait_bytes(qg_all.at[pl.ds(0, 3)], core_recv.at[0])
 
 
 def grads_kernel(
@@ -351,8 +368,8 @@
             pltpu.VMEM((1, 32), F32),
             pltpu.SMEM((1, 2), jnp.int32),
             pltpu.VMEM((32, 128), F32),
-            pltpu.VMEM((PSG, 32, 128), BF16),
-            pltpu.VMEM((PSG, 32, 128), F32),
+            pltpu.VMEM((2, PSG, 16, 128), BF16),
+            pltpu.VMEM((PSG, 16, 128), F32),
             pltpu.VMEM((1, 128), F32),
             pltpu.VMEM((PSG, 1, 128), F32),
             pltpu.VMEM(pieces, BF16),
@@ -373,8 +390,8 @@
             pltpu.VMEM((2, 32, 128), BF16),
             pltpu.VMEM((PB, 2, 32, 128), BF16),
             pltpu.SemaphoreType.DMA((10,)),
-            pltpu.SemaphoreType.DMA((8,)),
-            pltpu.SemaphoreType.DMA((9,)),
+            pltpu.SemaphoreType.DMA((10,)),
+            pltpu.SemaphoreType.DMA((11,)),
             pltpu.SemaphoreType.DMA((2,)),
             pltpu.SemaphoreType.DMA((5,)),
             pltpu.SemaphoreType.DMA((2,)),

time: 51.5 us -> 50.5 us (0.981)
  Pallas kernels: 50.7 us -> 49.7 us
    pallas_call x1, Pallas kernels: 46 us -> 44.9 us  [local(): pl.pallas_call(comm_kernel, out_shape=[sds((GROUPS, 512, 128), BF16), sds...]
where the time goes in v4:
time: 50.5 us; the launch traced here: 50.3 us
  Pallas kernels  49.7 us (98%)
  between operations  0.64 us (1%)
    pallas_call x1, Pallas kernels, local(): pl.pallas_call(comm_kernel, out_shape=[sds((GROUPS, 512, 128), BF16), sds...  44.9 us
    pallas_call x1, Pallas kernels, local(): pl.pallas_call(grads_kernel, out_shape=[sds((32, 128), BF16), sds((512, 2...  4.74 us

profile of v4, /device:TPU:1, one launch (start us, length us, event | category | flops | bytes accessed | tf_op | source)
XLA Modules:
  0.0 50.3 jit_solution(8383150708163364587)
XLA Ops:
  0.6 44.9 %comm.1 = (bf16[8,512,128]{2,1,0:T(8,128)(2,1)}, bf16[512,2048]{1,0:T(8,128)(2,1)}, f32[2048,128]{1,0:T(8,128)}, bf16[8,32,16,128]{3,2,1,0:T(8,128)(2,1)}, bf16[...) custom-call(bf16[32,128]{1,0:T(8,128)(2,1)} %bitcast.13, bf16[32,128]{1,0:T(8,128)(2,1)} %bitcast.14, ...), custom_call_target="tpu_custom_call" | custom-call | flops 1000000000 | bytes 10000000 | tf_op jit(solution)/shard_map/comm/pallas_call | solution.py:353
  45.6 4.7 %grads.1 = (bf16[32,128]{1,0:T(8,128)(2,1)}, bf16[512,2048]{1,0:T(8,128)(2,1)}, bf16[512,2048]{1,0:T(8,128)(2,1)}, f32[128,2048]{1,0:T(8,128)}, f32[2048,128]{1,0:T(8,128)}) custom-call(bf16[8,512,128]{2,1,0:T(8,128)(2,1)} %get-tuple-element.16.kgrad_in, bf16[512,2048]{1,0:T(8,128)(2,1)} %get-tuple-element.17.vgrad_in, ...), custom_call_target="tpu_custom_call" | custom-call | flops 1000000000 | bytes 10000000 | tf_op jit(solution)/shard_map/grads/pallas_call | solution.py:412

commit v5 on v4

--- a/solution.py
+++ b/solution.py
@@ -230,24 +230,6 @@
     for to in far_first:
         send(qg_all.at[opposite, me], qg_all.at[opposite, me], send_sem.at[6], recv_sem.at[8], (to, pb))
 
-    wait_bytes(o_all.at[pl.ds(0, 4)], x_recv.at[0])
-    tokens = jnp.concatenate([dg_all[s, 1] for s in range(PB)], axis=0)
-    for g in range(GROUPS):
-        rows = jnp.concatenate([columns(o_all[s, pl.ds(g * 4, 4)]) for s in range(PB)], axis=0)
-        owg[g * 256 : (g + 1) * 256, :] = dot(rows, tokens, TN)
-    owg_copy = pltpu.make_async_copy(owg, owg_out, out_sem.at[3])
-    owg_copy.start()
-    for i, count, ref in (
-        (0, PSG - 1, partial), (1, PSG - 1, qa.at[0]), (2, Y - 1, stats), (8, Y - 1, qa.at[1]), (9, PSG - Y, qa.at[1]), (3, PSG - 1, g_all), (4, PSG - 1, qpart),
-        (5, PSG - 1, qpart), (7, PSG - Y, stats),
-    ):
-        wait_bytes(ref.at[pl.ds(0, count)], send_sem.at[i])
-    wait_bytes(o_all.at[pl.ds(0, 7)], x_send.at[0])
-    wait_bytes(dg_all.at[pl.ds(0, PB - 1)], x_send.at[1])
-    wait_bytes(qg_own, side_send.at[0])
-    for copy in (vgrad_copy, kgrad_copy, dg_copy, owg_copy, q_copy):
-        copy.wait()
-
     def keep(at, first=0, count=PSG):
         part = pl.ds(first, count)
         pltpu.make_async_copy(qg_all.at[at, part], qg_out.at[at, part], out_sem.at[5]).start()
@@ -270,21 +252,42 @@
                     send(part, qg_out.at[slot, span], side_send.at[1], side_recv.at[2], (me, to))
     hand_over(slot, 0, PSG)
     keep(slot)
-    wait_bytes(qg_all.at[slot, pl.ds(0, PSG - 1)], recv_sem.at[8])
-    hand_over(opposite, 0, PSG)
-    keep(opposite)
+
+    wait_bytes(o_all.at[pl.ds(0, 4)], x_recv.at[0])
+    tokens = jnp.concatenate([dg_all[s, 1] for s in range(PB)], axis=0)
+    for g in range(GROUPS):
+        rows = jnp.concatenate([columns(o_all[s, pl.ds(g * 4, 4)]) for s in range(PB)], axis=0)
+        owg[g * 256 : (g + 1) * 256, :] = dot(rows, tokens, TN)
+    owg_copy = pltpu.make_async_copy(owg, owg_out, out_sem.at[3])
+    owg_copy.start()
+
+    for i, count, ref in (
+        (0, PSG - 1, partial), (1, PSG - 1, qa.at[0]), (2, Y - 1, stats), (8, Y - 1, qa.at[1]), (9, PSG - Y, qa.at[1]), (3, PSG - 1, g_all), (4, PSG - 1, qpart),
+        (5, PSG - 1, qpart), (7, PSG - Y, stats),
+    ):
+        wait_bytes(ref.at[pl.ds(0, count)], send_sem.at[i])
+    wait_bytes(o_all.at[pl.ds(0, 7)], x_send.at[0])
+    wait_bytes(dg_all.at[pl.ds(0, PB - 1)], x_send.at[1])
+    wait_bytes(qg_own, side_send.at[0])
+    for copy in (vgrad_copy, kgrad_copy, dg_copy, q_copy):
+        copy.wait()
+
     sides = [core * 4 + lax.rem(xpos + d, 4) for d in (3, 1)]
     wait_bytes(qg_all.at[slot], side_recv.at[1])
     for at in sides:
         hand_over(at, firsts[0], 16)
     for at in sides:
         keep(at, firsts[0], 16)
+    wait_bytes(qg_all.at[slot, pl.ds(0, PSG - 1)], recv_sem.at[8])
+    hand_over(opposite, 0, PSG)
+    keep(opposite)
     wait_bytes(qpart.at[pl.ds(0, PSG - 1)], send_sem.at[6])
     wait_bytes(qg_all.at[pl.ds(0, 3)], side_send.at[1])
     wait_bytes(qg_all.at[pl.ds(0, 3)], core_send.at[0])
     wait_bytes(qg_all.at[pl.ds(0, 3)], out_sem.at[5])
     wait_bytes(qg_all.at[pl.ds(0, 2)], side_recv.at[2])
     wait_bytes(qg_all.at[pl.ds(0, 3)], core_recv.at[0])
+    owg_copy.wait()
 
 
 def grads_kernel(

time: 50.5 us -> 50.7 us (level)
  no operation moved by 1% of the time
where the time goes in v5:
time: 50.7 us; the launch traced here: 50.5 us
  Pallas kernels  49.9 us (98%)
  between operations  0.64 us (1%)
    pallas_call x1, Pallas kernels, local(): pl.pallas_call(comm_kernel, out_shape=[sds((GROUPS, 512, 128), BF16), sds...  45.1 us
    pallas_call x1, Pallas kernels, local(): pl.pallas_call(grads_kernel, out_shape=[sds((32, 128), BF16), sds((512, 2...  4.77 us

profile of v5, /device:TPU:1, one launch (start us, length us, event | category | flops | bytes accessed | tf_op | source)
XLA Modules:
  0.0 50.5 jit_solution(2244455190147587738)
XLA Ops:
  0.6 45.1 %comm.1 = (bf16[8,512,128]{2,1,0:T(8,128)(2,1)}, bf16[512,2048]{1,0:T(8,128)(2,1)}, f32[2048,128]{1,0:T(8,128)}, bf16[8,32,16,128]{3,2,1,0:T(8,128)(2,1)}, bf16[...) custom-call(bf16[32,128]{1,0:T(8,128)(2,1)} %bitcast.13, bf16[32,128]{1,0:T(8,128)(2,1)} %bitcast.14, ...), custom_call_target="tpu_custom_call" | custom-call | flops 1000000000 | bytes 10000000 | tf_op jit(solution)/shard_map/comm/pallas_call | solution.py:356
  45.8 4.8 %grads.1 = (bf16[32,128]{1,0:T(8,128)(2,1)}, bf16[512,2048]{1,0:T(8,128)(2,1)}, bf16[512,2048]{1,0:T(8,128)(2,1)}, f32[128,2048]{1,0:T(8,128)}, f32[2048,128]{1,0:T(8,128)}) custom-call(bf16[8,512,128]{2,1,0:T(8,128)(2,1)} %get-tuple-element.16.kgrad_in, bf16[512,2048]{1,0:T(8,128)(2,1)} %get-tuple-element.17.vgrad_in, ...), custom_call_target="tpu_custom_call" | custom-call | flops 1000000000 | bytes 10000000 | tf_op jit(solution)/shard_map/grads/pallas_call | solution.py:415
